TPU v7x, 32 devices: a whole 2x2x4 slice. The times are simulated.
32 devices in a mesh: wide: 8 (over z, y), tensor: 4 (over x, core).
Axes of the slice: x: 2, y: 2, z: 4, core: 2. Of those that a mesh axis runs over, the one named last changes fastest.
Arguments:
- tokens: bfloat16 [8192, 768], P(('wide', 'tensor')), may hold values from -6 to 6
- cotangent: bfloat16 [8192, 768], P(('wide', 'tensor')), may hold values from -6 to 6
- gate_logits: float32 [8192, 2], P('wide'), may hold values from -4 to 4
- routes: int32 [8192, 2], P('wide'), may hold values from 0 to 7, all different within a row; in each aligned block of 256 rows (0 to 255, 256 to 511, ...) at most 128 rows name the same one
- parents: int32 [8, 13], P('wide'), may hold values from 0 to 12, as said below
- mixing_in: float32 [768, 2304], P(('wide', 'tensor')), may hold values from -0.21875 to 0.21875
- mixing_in_mean: float32 [768, 2304], P(('wide', 'tensor')), may hold values from -512 to 512
- mixing_in_square: float32 [768, 2304], P(('wide', 'tensor')), may hold values from 8192 to 32768
- mixing_out: float32 [768, 768], P(('wide', 'tensor')), may hold values from -1.75 to 1.75
- mixing_out_mean: float32 [768, 768], P(('wide', 'tensor')), may hold values from -80 to 80
- mixing_out_square: float32 [768, 768], P(('wide', 'tensor')), may hold values from 184.32 to 737.28
- norm_gains: float32 [2, 768], P(None, ('wide', 'tensor')), may hold values from 0.5 to 1.5
- norm_gains_mean: float32 [2, 768], P(None, ('wide', 'tensor')), may hold values from -1024 to 1024
- norm_gains_square: float32 [2, 768], P(None, ('wide', 'tensor')), may hold values from 32768 to 131072
- shared_in: float32 [768, 2, 2048], P('wide', None, 'tensor'), may hold values from -0.21875 to 0.21875
- shared_in_mean: float32 [768, 2, 2048], P('wide', None, 'tensor'), may hold values from -192 to 192
- shared_in_square: float32 [768, 2, 2048], P('wide', None, 'tensor'), may hold values from 1003.52 to 4014.08
- shared_out: float32 [2048, 768], P('tensor', 'wide'), may hold values from -0.125 to 0.125
- shared_out_mean: float32 [2048, 768], P('tensor', 'wide'), may hold values from -320 to 320
- shared_out_square: float32 [2048, 768], P('tensor', 'wide'), may hold values from 2949.12 to 11796.48
- expert_in: float32 [8, 768, 2, 2048], P('wide', None, None, 'tensor'), may hold values from -0.21875 to 0.21875
- expert_in_mean: float32 [8, 768, 2, 2048], P('wide', None, None, 'tensor'), may hold values from -48 to 48
- expert_in_square: float32 [8, 768, 2, 2048], P('wide', None, None, 'tensor'), may hold values from 59.1872 to 236.7488
- expert_out: float32 [8, 2048, 768], P('wide', 'tensor'), may hold values from -0.125 to 0.125
- expert_out_mean: float32 [8, 2048, 768], P('wide', 'tensor'), may hold values from -80 to 80
- expert_out_square: float32 [8, 2048, 768], P('wide', 'tensor'), may hold values from 184.32 to 737.28
Outputs:
- mixed: bfloat16 [8192, 768], P(('wide', 'tensor'))
- input_grad: float32 [8192, 768], P(('wide', 'tensor'))
- logit_grad: float32 [8192, 2], P(('wide', 'tensor'))
- mixing_in_mean_new: float32 [768, 2304], P(('wide', 'tensor'))
- mixing_in_square_new: float32 [768, 2304], P(('wide', 'tensor'))
- mixing_in_updated: float32 [768, 2304], P(('wide', 'tensor'))
- mixing_out_mean_new: float32 [768, 768], P(('wide', 'tensor'))
- mixing_out_square_new: float32 [768, 768], P(('wide', 'tensor'))
- mixing_out_updated: float32 [768, 768], P(('wide', 'tensor'))
- norm_gains_mean_new: float32 [2, 768], P(None, ('wide', 'tensor'))
- norm_gains_square_new: float32 [2, 768], P(None, ('wide', 'tensor'))
- norm_gains_updated: float32 [2, 768], P(None, ('wide', 'tensor'))
- shared_in_mean_new: float32 [768, 2, 2048], P('wide', None, 'tensor')
- shared_in_square_new: float32 [768, 2, 2048], P('wide', None, 'tensor')
- shared_in_updated: float32 [768, 2, 2048], P('wide', None, 'tensor')
- shared_out_mean_new: float32 [2048, 768], P('tensor', 'wide')
- shared_out_square_new: float32 [2048, 768], P('tensor', 'wide')
- shared_out_updated: float32 [2048, 768], P('tensor', 'wide')
- expert_in_mean_new: float32 [8, 768, 2, 2048], P('wide', None, None, 'tensor')
- expert_in_square_new: float32 [8, 768, 2, 2048], P('wide', None, None, 'tensor')
- expert_in_updated: float32 [8, 768, 2, 2048], P('wide', None, None, 'tensor')
- expert_out_mean_new: float32 [8, 2048, 768], P('wide', 'tensor')
- expert_out_square_new: float32 [8, 2048, 768], P('wide', 'tensor')
- expert_out_updated: float32 [8, 2048, 768], P('wide', 'tensor')
Inputs may be any that keep to these rules, and one draw needn't show every extreme that they name: `routes`: A token's 2 experts differ; in the rows of one device (aligned blocks of 256 tokens) no expert is named more than 128 times. `parents`: in each tree, entry 0 is 0; 4 of the other segments have parent 0 and each of them is the parent of exactly 2 segments.
All inputs are finite; a program needn't handle non-finite values.
Results may differ from a plain program's by a relative error of at most 0.019.
Values may be sent and summed in bfloat16 or wider, within the bound.
No kernel may reach another device: no remote copies, remote signals or barrier semaphores. Data moves between devices by JAX's collectives and lax.ppermute only.
A program may use at most 256 MiB of HBM per device.

v0:
```python
import functools
import math

import jax
import jax.numpy as jnp
from jax import lax
from jax.experimental import pallas as pl
from jax.experimental.pallas import tpu as pltpu
from jax.sharding import PartitionSpec as P

HEAD = 64
TOP = 2
TRUNK = 256
SEG = 64
STEP = 5
SEGS = 13


NORM_EPS = 1e-06
BETA_ONE = 0.5
BETA_TWO = 0.5
ADAM_EPS = 1e-08
DECAY = 0.01
RATES = (0.02, 0.15, 0.3, 0.02, 0.012, 0.02, 0.012)

LOW = jnp.bfloat16
FULL = jnp.float32
SMALL = pl.CostEstimate(flops=1000, bytes_accessed=1000, transcendentals=0)


def dot(a, b):
    return jnp.dot(a, b, preferred_element_type=FULL)


def dot_nt(a, b):
    return lax.dot_general(a, b, (((1,), (1,)), ((), ())), preferred_element_type=FULL)


def dot_tn(a, b):
    return lax.dot_general(a, b, (((0,), (0,)), ((), ())), preferred_element_type=FULL)


def rms_factor(values):
    return lax.rsqrt(jnp.mean(values * values, axis=-1, keepdims=True) + NORM_EPS)


def rms_back(values, factor, gain, grad):
    hat = values * factor
    scaled = grad * gain
    return factor * (scaled - hat * jnp.mean(scaled * hat, axis=-1, keepdims=True)), hat


def rotary_tables(position):
    half = HEAD // 2
    frequency = 10000.0 ** (-jnp.arange(half, dtype=FULL) / half)
    angles = position[:, None] * frequency[None, :]
    return jnp.cos(angles)[:, None, :], jnp.sin(angles)[:, None, :]


def rotate(values, cosine, sine):
    half = values.shape[-1] // 2
    one, two = values[..., :half], values[..., half:]
    return jnp.concatenate([one * cosine - two * sine, two * cosine + one * sine], axis=-1)


def tree_layout(parent_row, places):
    segment = jnp.where(places < TRUNK, 0, 1 + (places - TRUNK) // SEG)
    seg_start = jnp.where(segment == 0, 0, TRUNK + (segment - 1) * SEG)
    matches = segment[:, None] == jnp.arange(SEGS, dtype=jnp.int32)[None, :]
    upward = jnp.sum(jnp.where(matches, parent_row[None, :], 0), axis=1)
    depth_base = jnp.where(upward == 0, TRUNK, TRUNK + SEG)
    position = jnp.where(segment == 0, places, depth_base + places - seg_start)
    return (segment, upward, position)


def allowed_mask(segment, upward, places):
    same_segment = (segment[None, :] == segment[:, None]) & (places[None, :] <= places[:, None])
    ancestor = (segment[:, None] != 0) & (
        (segment[None, :] == 0) | (segment[None, :] == upward[:, None])
    )
    return same_segment | ancestor


def attend_forward(queries, keys, values, allowed):
    scale = 1.0 / math.sqrt(HEAD)
    scores = jnp.einsum("qhd,khd->hqk", queries, keys, preferred_element_type=FULL) * scale
    scores = jnp.where(allowed[None], scores, -1e30)
    row_top = jnp.max(scores, axis=-1, keepdims=True)
    shifted = jnp.exp(scores - row_top)
    row_total = jnp.sum(shifted, axis=-1, keepdims=True)
    weights = (shifted / row_total).astype(LOW)
    attended = jnp.einsum("hqk,khd->qhd", weights, values, preferred_element_type=FULL)
    return attended, row_top + jnp.log(row_total)


def attend_backward(queries, keys, values, allowed, grad_attended, log_totals):
    scale = 1.0 / math.sqrt(HEAD)
    scores = jnp.einsum("qhd,khd->hqk", queries, keys, preferred_element_type=FULL) * scale
    scores = jnp.where(allowed[None], scores, -1e30)
    probs = jnp.exp(scores - log_totals)
    grad_probs = jnp.einsum("qhd,khd->hqk", grad_attended, values, preferred_element_type=FULL)
    inner = jnp.sum(probs * grad_probs, axis=-1, keepdims=True)
    grad_scores = (probs * (grad_probs - inner)).astype(LOW)
    grad_query = jnp.einsum("hqk,khd->qhd", grad_scores, keys, preferred_element_type=FULL) * scale
    grad_key = jnp.einsum("hqk,qhd->khd", grad_scores, queries, preferred_element_type=FULL) * scale
    grad_value = jnp.einsum(
        "hqk,qhd->khd", probs.astype(LOW), grad_attended, preferred_element_type=FULL
    )
    return grad_query, grad_key, grad_value


def branch_rows_kernel(chunks, x_ref, g_ref, *refs):
    weights = refs[:chunks]
    hidden_ref, ggate_ref, gup_ref, grad_ref, xt_ref, gt_ref = refs[chunks:]
    x, g = x_ref[...], g_ref[...]
    xt_ref[...] = x.T
    gt_ref[...] = g.T
    total = None
    for chunk in range(chunks):
        w = weights[chunk]
        size = w.shape[2]
        at = pl.ds(chunk * size, size)
        gate, up, grad_hidden = dot(x, w[0]), dot(x, w[1]), dot(g, w[2])
        sigmoid = 1.0 / (1.0 + jnp.exp(-gate))
        active = gate * sigmoid
        hidden_ref[:, at] = (active * up).astype(LOW)
        ggate = (grad_hidden * up * sigmoid * (1.0 + gate * (1.0 - sigmoid))).astype(LOW)
        gup = (grad_hidden * active).astype(LOW)
        ggate_ref[:, at] = ggate
        gup_ref[:, at] = gup
        part = dot_nt(ggate, w[0]) + dot_nt(gup, w[1])
        total = part if total is None else total + part
    grad_ref[...] = total.astype(LOW)


def branch_rows(x, g, chunks):
    rows, width = x.shape
    size = chunks[0].shape[2]
    hidden = size * len(chunks)
    block = math.gcd(rows, 256)
    row_spec = pl.BlockSpec((block, width), lambda i: (i, 0))
    hidden_spec = pl.BlockSpec((block, hidden), lambda i: (i, 0))
    whole = [
        pl.BlockSpec(w.shape, lambda i: (0, 0, 0), pipeline_mode=pl.Buffered(1)) for w in chunks
    ]
    hidden_type = jax.ShapeDtypeStruct((rows, hidden), LOW)
    turned_spec = pl.BlockSpec((width, block), lambda i: (0, i))
    turned_type = jax.ShapeDtypeStruct((width, rows), LOW)
    return pl.pallas_call(
        functools.partial(branch_rows_kernel, len(chunks)),
        grid=(rows // block,),
        in_specs=[row_spec, row_spec] + whole,
        out_specs=[hidden_spec] * 3 + [row_spec] + [turned_spec] * 2,
        out_shape=[hidden_type] * 3
        + [jax.ShapeDtypeStruct((rows, width), LOW)]
        + [turned_type] * 2,
        compiler_params=pltpu.CompilerParams(vmem_limit_bytes=48 * 1024 * 1024),
        cost_estimate=SMALL,
        name="branch_rows",
    )(x, g, *chunks)


def branch_out_kernel(chunks, hidden_ref, *refs):
    weights, out_ref = refs[:chunks], refs[chunks]
    total = None
    for chunk in range(chunks):
        w_out = weights[chunk][0]
        size = w_out.shape[1]
        part = dot_nt(hidden_ref[:, pl.ds(chunk * size, size)], w_out)
        total = part if total is None else total + part
    out_ref[...] = total.astype(LOW)


def branch_out(hidden, chunks):
    rows, size = hidden.shape
    width = chunks[0].shape[1]
    block = math.gcd(rows, 256)
    return pl.pallas_call(
        functools.partial(branch_out_kernel, len(chunks)),
        grid=(rows // block,),
        in_specs=[pl.BlockSpec((block, size), lambda i: (i, 0))]
        + [
            pl.BlockSpec(
                (1,) + w.shape[1:], lambda i: (2, 0, 0), pipeline_mode=pl.Buffered(1)
            )
            for w in chunks
        ],
        out_specs=pl.BlockSpec((block, width), lambda i: (i, 0)),
        out_shape=jax.ShapeDtypeStruct((rows, width), LOW),
        compiler_params=pltpu.CompilerParams(vmem_limit_bytes=48 * 1024 * 1024),
        cost_estimate=SMALL,
        name="branch_out",
    )(hidden, *chunks)


def branch_grads_kernel(xt_ref, gt_ref, hidden_ref, ggate_ref, gup_ref, grad_ref):
    xt = xt_ref[...]
    grad_ref[0, 0] = dot(xt, ggate_ref[...]).astype(LOW)
    grad_ref[0, 1] = dot(xt, gup_ref[...]).astype(LOW)
    grad_ref[0, 2] = dot(gt_ref[...], hidden_ref[...]).astype(LOW)


def branch_grads(turned, states, first, chunks, size):
    width, rows = turned[0].shape
    block = math.gcd(width, 256)
    turned_spec = pl.BlockSpec((block, rows), lambda j, i: (i, 0))
    hidden_spec = pl.BlockSpec((rows, size), lambda j, i: (0, first + j))
    return pl.pallas_call(
        branch_grads_kernel,
        grid=(chunks, width // block),
        in_specs=[turned_spec] * 2 + [hidden_spec] * 3,
        out_specs=pl.BlockSpec((1, 3, block, size), lambda j, i: (j, 0, i, 0)),
        out_shape=jax.ShapeDtypeStruct((chunks, 3, width, size), LOW),
        compiler_params=pltpu.CompilerParams(vmem_limit_bytes=48 * 1024 * 1024),
        cost_estimate=SMALL,
        name="branch_grads",
    )(*turned, *states)


def adam_step(weight, mean_old, square_old, gradient, rate):
    mean_new = BETA_ONE * mean_old + (1.0 - BETA_ONE) * gradient
    square_new = BETA_TWO * square_old + (1.0 - BETA_TWO) * gradient * gradient
    mean_hat = mean_new / (1.0 - BETA_ONE**STEP)
    square_hat = square_new / (1.0 - BETA_TWO**STEP)
    updated = weight - rate * (mean_hat / (jnp.sqrt(square_hat) + ADAM_EPS) + DECAY * weight)
    return (mean_new, square_new, updated)


def shared_grads_kernel(xt_ref, gt_ref, hidden_ref, ggate_ref, gup_ref, grad_ref):
    groups, _, rows, _ = grad_ref.shape
    for plane, (turned, state) in enumerate(
        ((xt_ref, ggate_ref), (xt_ref, gup_ref), (gt_ref, hidden_ref))
    ):
        grad = dot(turned[...], state[...])
        for group in range(groups):
            grad_ref[group, plane] = grad[group * rows : (group + 1) * rows].astype(LOW)


def shared_grads(turned, states, wide):
    width, rows = turned[0].shape
    size = states[0].shape[1]
    share = width // wide
    groups = max(g for g in range(1, wide + 1) if wide % g == 0 and g * share <= 384)
    turned_spec = pl.BlockSpec((groups * share, rows), lambda i: (i, 0))
    return pl.pallas_call(
        shared_grads_kernel,
        grid=(wide // groups,),
        in_specs=[turned_spec] * 2 + [pl.BlockSpec((rows, size), lambda i: (0, 0))] * 3,
        out_specs=pl.BlockSpec((groups, 3, share, size), lambda i: (i, 0, 0, 0)),
        out_shape=jax.ShapeDtypeStruct((wide, 3, share, size), LOW),
        compiler_params=pltpu.CompilerParams(vmem_limit_bytes=48 * 1024 * 1024),
        cost_estimate=SMALL,
        name="shared_grads",
    )(*turned, *states)


def sum_of(refs, plane):
    total = refs[0][0, plane].astype(FULL)
    for ref in refs[1:]:
        total = total + ref[0, plane].astype(FULL)
    return total


def adam_in_kernel(count, rate, *refs):
    parts, (w_ref, mean_ref, square_ref), outs = refs[:count], refs[count : count + 3], refs[-4:-1]
    grad_ref = refs[-1]
    _, _, rows, size = parts[0].shape
    tiles = size // 128
    for half in range(2):
        total = sum_of(parts, half)
        for tile in range(tiles):
            at = pl.ds(2 * tile + half, rows, 2 * tiles)
            grad_ref[at, :] = total[:, tile * 128 : (tile + 1) * 128]
    results = adam_step(w_ref[...], mean_ref[...], square_ref[...], grad_ref[...], rate)
    for ref, value in zip(outs, results):
        ref[...] = value


def adam_in(parts, weight, mean, square, rate):
    _, width, _, size = weight.shape
    tiles = size // 128
    block = math.gcd(width, 128)

    def rows_of(value):
        value = value[0].reshape(width, 2, tiles, 128).transpose(0, 2, 1, 3)
        return value.reshape(width * 2 * tiles, 128)

    spec = pl.BlockSpec((block * 2 * tiles, 128), lambda i: (i, 0))
    outs = pl.pallas_call(
        functools.partial(adam_in_kernel, len(parts), rate),
        grid=(width // block,),
        in_specs=[pl.BlockSpec((1, 2, block, size), lambda i: (0, 0, i, 0))] * len(parts) + [spec] * 3,
        out_specs=[spec] * 3,
        out_shape=[jax.ShapeDtypeStruct((width * 2 * tiles, 128), FULL)] * 3,
        scratch_shapes=[pltpu.VMEM((block * 2 * tiles, 128), FULL)],
        compiler_params=pltpu.CompilerParams(vmem_limit_bytes=48 * 1024 * 1024),
        cost_estimate=SMALL,
        name="adam_in",
    )(*parts, rows_of(weight), rows_of(mean), rows_of(square))
    return [
        out.reshape(width, tiles, 2, 128).transpose(0, 2, 1, 3).reshape(weight.shape)
        for out in outs
    ]


def adam_out_kernel(count, rate, *refs):
    parts, (w_ref, mean_ref, square_ref), outs = refs[:count], refs[count : count + 3], refs[-3:]
    total = sum_of(parts, 0).T
    results = adam_step(w_ref[0], mean_ref[0], square_ref[0], total, rate)
    for ref, value in zip(outs, results):
        ref[0] = value


def adam_out(parts, weight, mean, square, rate):
    _, size, width = weight.shape
    block = math.gcd(width, 128)
    spec = pl.BlockSpec((1, size, block), lambda i: (0, 0, i))
    last = [
        pl.BlockSpec((1, 1, block, size), functools.partial(lambda n, i: (0, n, i, 0), p.shape[1] - 1))
        for p in parts
    ]
    return pl.pallas_call(
        functools.partial(adam_out_kernel, len(parts), rate),
        grid=(width // block,),
        in_specs=last + [spec] * 3,
        out_specs=[spec] * 3,
        out_shape=[jax.ShapeDtypeStruct(weight.shape, FULL)] * 3,
        compiler_params=pltpu.CompilerParams(vmem_limit_bytes=48 * 1024 * 1024),
        cost_estimate=SMALL,
        name="adam_out",
    )(*parts, weight, mean, square)


def swap(value, axis, mask, count):
    return lax.ppermute(value, axis, [(i, i ^ mask) for i in range(count)])


def after(value, *earlier):
    return lax.optimization_barrier((value,) + earlier)[0]


def by_rank(parts, rank):
    count = len(parts)
    ordered = []
    for place in range(count):
        chosen = parts[place]
        for other in range(1, count):
            chosen = jnp.where(rank == other, parts[place ^ other], chosen)
        ordered.append(chosen)
    return ordered


def gather_relative(value, count):
    if count != 4:
        rank = lax.axis_index("tensor")
        every = lax.all_gather(value, "tensor", axis=0)
        return [lax.dynamic_index_in_dim(every, rank ^ m, 0, False) for m in range(count)]
    far = swap(value, "tensor", 2, count)
    near = swap(value, "tensor", 1, count)
    return [value, near, far, swap(far, "tensor", 1, count)]


def send_relative(parts):
    count = len(parts)
    return [parts[0]] + [swap(parts[m], "tensor", m, count) for m in range(1, count)]


def sum_relative(parts):
    got = send_relative([p.astype(LOW) for p in parts])
    total = parts[0].astype(FULL)
    for part in got[1:]:
        total = total + part.astype(FULL)
    return total


def block_of(value, place, size, dim=0):
    return lax.dynamic_slice_in_dim(value, place * size, size, dim)


def exchange(value):
    return lax.all_to_all(value, "wide", split_axis=0, concat_axis=0, tiled=True)


def body(
    tokens,
    cotangent,
    gate_logits,
    routes,
    parents,
    mixing_in,
    mixing_in_mean,
    mixing_in_square,
    mixing_out,
    mixing_out_mean,
    mixing_out_square,
    norm_gains,
    norm_gains_mean,
    norm_gains_square,
    shared_in,
    shared_in_mean,
    shared_in_square,
    shared_out,
    shared_out_mean,
    shared_out_square,
    expert_in,
    expert_in_mean,
    expert_in_square,
    expert_out,
    expert_out_mean,
    expert_out_square,
):
    rows_dev, width = tokens.shape
    wide = lax.axis_size("wide")
    count = lax.axis_size("tensor")
    rank = lax.axis_index("tensor")
    tree_length = rows_dev * count
    capacity = 2 * rows_dev * TOP // wide
    slots = wide * capacity
    heads = width // HEAD
    heads_dev = -(-heads // count)
    head_pad = heads_dev * count - heads
    head_width = heads_dev * HEAD
    rows_weight = mixing_in.shape[0]

    cut = mixing_in.astype(LOW).reshape(rows_weight, 3, heads, HEAD)
    cut = jnp.pad(cut, ((0, 0), (0, 0), (0, head_pad), (0, 0)))
    cut = cut.reshape(rows_weight, 3, count, head_width).transpose(2, 0, 1, 3)
    cut = cut.reshape(count, rows_weight, 3 * head_width)
    gain_columns = jnp.broadcast_to(norm_gains.astype(LOW).T[None], (count, rows_weight, 2))
    cut = jnp.concatenate([cut, gain_columns], axis=2)
    sent = jnp.broadcast_to(cut[None], (wide,) + cut.shape).reshape(
        wide * count, rows_weight, 3 * head_width + 2
    )
    got = lax.all_to_all(sent, ("wide", "tensor"), split_axis=0, concat_axis=0, tiled=True)
    got = got.reshape(width, 3 * head_width + 2)
    w_qkv = got[:, : 3 * head_width]
    gain_pair = got[:, 3 * head_width :].astype(FULL).T

    token_parts = gather_relative(tokens, count)
    tokens_all = jnp.concatenate(by_rank(token_parts, rank), axis=0)
    expert_low = jnp.concatenate(
        [expert_in[0].astype(LOW).transpose(1, 0, 2), expert_out.astype(LOW).transpose(0, 2, 1)],
        axis=0,
    )
    expert_chunks = gather_relative(expert_low, count)
    if count == 4:
        expert_chunks = [expert_chunks[m] for m in (0, 2, 1, 3)]
    shared_low = jnp.concatenate(
        [shared_in.astype(LOW).transpose(1, 0, 2), shared_out.astype(LOW).T[None]], axis=0
    )
    w_mix_out = lax.all_gather(mixing_out.astype(LOW), ("wide", "tensor"), axis=0, tiled=True)
    shared_low = after(shared_low, w_mix_out)
    w_shared = lax.all_gather(shared_low, "wide", axis=1, tiled=True)

    own_routes = lax.dynamic_slice_in_dim(routes, rank * rows_dev, rows_dev, 0)
    own_logits = lax.dynamic_slice_in_dim(gate_logits, rank * rows_dev, rows_dev, 0)
    gates = jax.nn.softmax(own_logits, axis=-1)
    flat = own_routes.reshape(-1)
    named = (flat[:, None] == jnp.arange(wide, dtype=jnp.int32)[None, :]).astype(LOW)
    order = jnp.arange(flat.shape[0], dtype=jnp.int32)
    earlier = (order[None, :] < order[:, None]).astype(LOW)
    before = jnp.sum(dot(earlier, named) * named.astype(FULL), axis=1).astype(jnp.int32)
    places = (flat * capacity + before).reshape(rows_dev, TOP)
    slot_ids = jnp.arange(slots, dtype=jnp.int32)
    picks = [(slot_ids[:, None] == places[:, k][None, :]).astype(LOW) for k in range(TOP)]
    pick_any = picks[0] + picks[1]
    grad_out = cotangent.astype(FULL)
    grad_routes = [(gates[:, k : k + 1] * grad_out).astype(LOW) for k in range(TOP)]
    grad_slots = (dot(picks[0], grad_routes[0]) + dot(picks[1], grad_routes[1])).astype(LOW)
    grad_slots = after(grad_slots, got)
    expert_grads = exchange(grad_slots.reshape(wide, capacity, width)).reshape(slots, width)

    tree_places = jnp.arange(tree_length, dtype=jnp.int32)
    segment, upward, position = tree_layout(parents[0], tree_places)
    allowed = allowed_mask(segment, upward, tree_places)
    cosine, sine = rotary_tables(position.astype(FULL))
    tree_rows = tokens_all.astype(FULL)
    normed_one = (tree_rows * rms_factor(tree_rows) * gain_pair[0]).astype(LOW)
    projected = dot(normed_one, w_qkv).reshape(tree_length, 3, heads_dev, HEAD)
    queries = rotate(projected[:, 0], cosine, sine).astype(LOW)
    keys = rotate(projected[:, 1], cosine, sine).astype(LOW)
    values = projected[:, 2].astype(LOW)
    attended, log_totals = attend_forward(queries, keys, values, allowed)
    attended = attended.astype(LOW).reshape(tree_length, head_width)
    attended_own = attended
    attended = send_relative([block_of(attended, rank ^ m, rows_dev) for m in range(count)])
    attended_low = jnp.concatenate(by_rank(attended, rank), axis=1)[:, :width]
    attended_low = after(attended_low, expert_chunks[1])
    input_rows = tokens.astype(FULL)
    residual = input_rows + dot(attended_low, w_mix_out)
    factor_two = rms_factor(residual)
    normed_two = (residual * factor_two * gain_pair[1]).astype(LOW)

    row_slots = dot(pick_any, normed_two).astype(LOW)
    row_slots = after(row_slots, expert_grads)
    expert_rows = exchange(row_slots.reshape(wide, capacity, width)).reshape(slots, width)
    shared_rows = jnp.concatenate(gather_relative(normed_two, count), axis=0)
    cotangent_late = after(cotangent, normed_two)
    cotangent_rel = jnp.concatenate(gather_relative(cotangent_late, count), axis=0)
    expert_rows, shared_rows, cotangent_rel = lax.optimization_barrier(
        (expert_rows, shared_rows, cotangent_rel)
    )

    *ex_states, ex_grad_rows, ex_xt, ex_gt = branch_rows(expert_rows, expert_grads, expert_chunks)
    back_rows = exchange(ex_grad_rows.reshape(wide, capacity, width)).reshape(slots, width)
    shared_rows = after(shared_rows, ex_grad_rows)
    *sh_states, sh_grad_rows, sh_xt, sh_gt = branch_rows(shared_rows, cotangent_rel, [w_shared])
    ex_states = list(after(tuple(ex_states), sh_grad_rows))
    sh_grad_rows = sum_relative(jnp.split(sh_grad_rows, count))
    sh_part = branch_out(sh_states[0], [w_shared])
    sh_part = sum_relative(jnp.split(sh_part, count))
    sh_size = sh_states[0].shape[1]
    sh_grads = shared_grads((sh_xt, sh_gt), sh_states, wide)
    rows_shared = width // wide
    ex_size = ex_states[0].shape[1] // count
    ex_grads = functools.partial(branch_grads, (ex_xt, ex_gt), ex_states)
    if count == 4:
        ex_sent = swap(ex_grads(2, 2, ex_size), "tensor", 1, count)
        ex_kept = ex_grads(0, 2, ex_size)
    else:
        ex_sent, ex_kept = (), ex_grads(0, count, ex_size)
    out_rows = branch_out(ex_states[0], expert_chunks)
    back_rows, out_rows, ex_kept, sh_grads, sh_part = lax.optimization_barrier(
        (back_rows, out_rows, ex_kept, sh_grads, sh_part)
    )
    returned = exchange(out_rows.reshape(wide, capacity, width)).reshape(slots, width)

    grad_normed_two = dot_tn(pick_any, back_rows) + sh_grad_rows
    grad_part, hat_two = rms_back(residual, factor_two, gain_pair[1], grad_normed_two)
    gain_two_part = jnp.sum(grad_normed_two * hat_two, axis=0)
    grad_residual = grad_out + grad_part
    grad_res_low = grad_residual.astype(LOW)
    w_mix_pad = jnp.pad(w_mix_out, ((0, head_pad * HEAD), (0, 0)))
    grad_res_parts = gather_relative(grad_res_low, count)
    grad_res_all = jnp.concatenate(by_rank(grad_res_parts, rank), axis=0)
    w_mix_own = block_of(w_mix_pad, rank, head_width)
    grad_attended = dot_nt(grad_res_all, w_mix_own).astype(LOW)
    grad_attended = grad_attended.reshape(tree_length, heads_dev, HEAD)
    if head_width == rows_weight * wide:
        grad_mix_out = dot_tn(attended_own, grad_res_all).astype(LOW)
        lines = rows_weight * width // sh_size
        sums = jnp.concatenate(
            [
                sh_grads.reshape(wide, 3 * rows_shared, sh_size),
                grad_mix_out.reshape(wide, lines, sh_size),
            ],
            axis=1,
        )
        grad_attended, sums = lax.optimization_barrier((grad_attended, sums))
        sums = lax.psum_scatter(sums, "wide", scatter_dimension=0, tiled=True)[0]
        turns = [(w * count + t, t * wide + w) for w in range(wide) for t in range(count)]
    else:
        grad_mix_out = dot_tn(attended_low, grad_res_low).astype(LOW)
        sums = lax.all_to_all(
            grad_mix_out.reshape(wide * count, rows_weight, width),
            ("wide", "tensor"),
            split_axis=0,
            concat_axis=0,
            tiled=True,
        )
        sh_grads = lax.psum_scatter(sh_grads, "wide", scatter_dimension=0, tiled=True)
        turns = None
    across = ()
    if count == 4:
        across = ex_kept[1].astype(FULL) + ex_sent[1].astype(FULL)
        across = across.astype(LOW)
        across_in, across_out, grad_attended = lax.optimization_barrier(
            (across[:2], across[2:], grad_attended)
        )
        across_in = swap(across_in, "tensor", 2, count)
        across_out = swap(after(across_out, across_in), "tensor", 2, count)
        across = (across_in,)

    grad_query, grad_key, grad_value = attend_backward(
        queries, keys, values, allowed, grad_attended, log_totals
    )
    grad_projected = jnp.stack(
        [rotate(grad_query, cosine, -sine), rotate(grad_key, cosine, -sine), grad_value], axis=1
    )
    grad_projected = grad_projected.astype(LOW).reshape(tree_length, 3 * head_width)
    grad_normed_one = dot_nt(grad_projected, w_qkv).astype(LOW)
    row_grads = send_relative(
        [block_of(grad_normed_one, rank ^ m, rows_dev) for m in range(count)]
    )
    grad_mix_in = dot_tn(normed_one, grad_projected).astype(LOW)
    grad_mix_in = after(grad_mix_in, returned, *across)
    if count == 4:
        in_parts = [ex_kept, ex_sent, across_in[None]]
        out_parts = [ex_kept, ex_sent, after(across_out, grad_projected)[None]]
    else:
        in_parts = [part[None] for part in send_relative([ex_kept[m] for m in range(count)])]
        out_parts = in_parts
    returned = after(returned, grad_projected)
    sent = jnp.concatenate([grad_mix_in, gain_two_part.astype(LOW)[:, None]], axis=1)
    got = lax.all_to_all(
        sent.reshape(wide * count, rows_weight, 3 * head_width + 1),
        ("wide", "tensor"),
        split_axis=0,
        concat_axis=0,
        tiled=True,
    )
    row_grads, sums, sh_grads = after((row_grads, sums, sh_grads), got)
    grad_normed_one = sum(part.astype(FULL) for part in row_grads)
    if turns:
        sh_grads = sums[: 3 * rows_shared].reshape(3, rows_shared, sh_size).astype(FULL)
        grad_mix_out = sums[3 * rows_shared :].reshape(rows_weight, width)
        grad_mix_out = lax.ppermute(grad_mix_out, ("wide", "tensor"), turns).astype(FULL)
    else:
        sh_grads = sh_grads[0].astype(FULL)
        grad_mix_out = jnp.sum(sums.astype(FULL), axis=0)
    got = jnp.sum(got.astype(FULL).reshape(wide, count, rows_weight, -1), axis=0)
    grad_gain_two = jnp.sum(got[:, :, 3 * head_width], axis=0)
    grad_mix_in = got[:, :, : 3 * head_width].reshape(count, rows_weight, 3, head_width)
    grad_mix_in = grad_mix_in.transpose(1, 2, 0, 3).reshape(rows_weight, 3, count * head_width)
    grad_mix_in = grad_mix_in[:, :, :width].reshape(rows_weight, 3 * width)
    grad_gain_one = jnp.sum(mixing_in.astype(LOW).astype(FULL) * grad_mix_in, axis=1)
    grad_gain_one = grad_gain_one / norm_gains[0].astype(LOW).astype(FULL)

    grad_part, _ = rms_back(input_rows, rms_factor(input_rows), gain_pair[0], grad_normed_one)
    input_grad = grad_residual + grad_part

    per_route = [dot_tn(picks[k], returned) for k in range(TOP)]
    mixed = residual + gates[:, :1] * per_route[0] + gates[:, 1:] * per_route[1]
    mixed = mixed + sh_part
    gate_grad = jnp.stack([jnp.sum(grad_out * rows, axis=-1) for rows in per_route], axis=1)
    logit_grad = gates * (gate_grad - jnp.sum(gates * gate_grad, axis=-1, keepdims=True))

    gradients = (
        (mixing_in, mixing_in_mean, mixing_in_square, grad_mix_in),
        (mixing_out, mixing_out_mean, mixing_out_square, grad_mix_out),
        (
            norm_gains,
            norm_gains_mean,
            norm_gains_square,
            jnp.stack([grad_gain_one, grad_gain_two]),
        ),
        (shared_in, shared_in_mean, shared_in_square, sh_grads[:2].transpose(1, 0, 2)),
        (shared_out, shared_out_mean, shared_out_square, sh_grads[2].T),
    )
    results = [mixed.astype(LOW), input_grad, logit_grad]
    for number, (weight, mean, square, gradient) in enumerate(gradients):
        results.extend(adam_step(weight, mean, square, gradient, RATES[number]))
    results.extend(adam_in(in_parts, expert_in, expert_in_mean, expert_in_square, RATES[5]))
    results.extend(adam_out(out_parts, expert_out, expert_out_mean, expert_out_square, RATES[6]))
    return tuple(results)


def solution(mesh):
    placed = (
        P(("wide", "tensor"), None),
        P(("wide", "tensor"), None),
        P("wide", None),
        P("wide", None),
        P("wide", None),
        P(("wide", "tensor"), None),
        P(("wide", "tensor"), None),
        P(("wide", "tensor"), None),
        P(("wide", "tensor"), None),
        P(("wide", "tensor"), None),
        P(("wide", "tensor"), None),
        P(None, ("wide", "tensor")),
        P(None, ("wide", "tensor")),
        P(None, ("wide", "tensor")),
        P("wide", None, "tensor"),
        P("wide", None, "tensor"),
        P("wide", None, "tensor"),
        P("tensor", "wide"),
        P("tensor", "wide"),
        P("tensor", "wide"),
        P("wide", None, None, "tensor"),
        P("wide", None, None, "tensor"),
        P("wide", None, None, "tensor"),
        P("wide", "tensor", None),
        P("wide", "tensor", None),
        P("wide", "tensor", None),
    )
    return jax.shard_map(
        body,
        mesh=mesh,
        in_specs=placed,
        out_specs=(
            P(("wide", "tensor"), None),
            P(("wide", "tensor"), None),
            P(("wide", "tensor"), None),
            P(("wide", "tensor"), None),
            P(("wide", "tensor"), None),
            P(("wide", "tensor"), None),
            P(("wide", "tensor"), None),
            P(("wide", "tensor"), None),
            P(("wide", "tensor"), None),
            P(None, ("wide", "tensor")),
            P(None, ("wide", "tensor")),
            P(None, ("wide", "tensor")),
            P("wide", None, "tensor"),
            P("wide", None, "tensor"),
            P("wide", None, "tensor"),
            P("tensor", "wide"),
            P("tensor", "wide"),
            P("tensor", "wide"),
            P("wide", None, None, "tensor"),
            P("wide", None, None, "tensor"),
            P("wide", None, None, "tensor"),
            P("wide", "tensor", None),
            P("wide", "tensor", None),
            P("wide", "tensor", None),
        ),
        check_vma=False,
    )
```

profile of v0, /device:TPU:3, one launch (start us, length us, event | category | flops | bytes accessed | tf_op | source)
XLA Modules:
  0.0 419.8 jit_solution(14055791662697743225)
XLA Ops:
  11.4 6.5 %all-to-all-start = ((bf16[32,24,578]{2,1,0:T(8,128)(2,1)}), bf16[32,24,578]{2,1,0:T(8,128)(2,1)}, u32[]{:S(2)}, u32[]{:S(2)}) async-start(bf16[32,24,578]{2,1,0:T(8,128)(2,1)} %bitcast.148), calls=%async_computation | async-start | bytes 1966080 | tf_op jit(solution)/shard_map/all_to_all | solution.py:434
  49.9 4.8 %all-to-all-start.1 = ((bf16[8,128,768]{2,1,0:T(8,128)(2,1)}), bf16[8,128,768]{2,1,0:T(8,128)(2,1)}, u32[]{:S(2)}, u32[]{:S(2)}) async-start(bf16[8,128,768]{2,1,0:T(8,128)(2,1)} %bitcast.145), calls=%async_computation.1 | async-start | bytes 3145728 | tf_op jit(solution)/shard_map/all_to_all | solution.py:381
  73.4 13.6 %collective-permute-done.3 = bf16[256,192]{0,1:T(8,128)(2,1)S(1)} collective-permute-done((bf16[256,192]{0,1:T(8,128)(2,1)}, bf16[256,192]{0,1:T(8,128)(2,1)S(1)}, u32[]{:S(2)}, u32[]{:S(2)}) %collective-permute-start.3) | collective-permute-done | bytes 98336 | tf_op jit(solution)/shard_map/ppermute | solution.py:335
  99.0 6.0 %all-to-all-start.2 = ((bf16[8,128,768]{2,1,0:T(8,128)(2,1)}), bf16[8,128,768]{2,1,0:T(8,128)(2,1)}, u32[]{:S(2)}, u32[]{:S(2)}) async-start(bf16[8,128,768]{2,1,0:T(8,128)(2,1)} %bitcast.158), calls=%async_computation.2 | async-start | bytes 3145728 | tf_op jit(solution)/shard_map/all_to_all | solution.py:381
  107.9 8.2 %collective-permute-done.11 = bf16[256,768]{1,0:T(8,128)(2,1)S(1)} collective-permute-done((bf16[256,768]{1,0:T(8,128)(2,1)S(1)}, bf16[256,768]{1,0:T(8,128)(2,1)S(1)}, u32[]{:S(2)}, u32[]{:S(2)}) %collective-permute-start.11) | collective-permute-done | bytes 393248 | tf_op jit(solution)/shard_map/ppermute | solution.py:335
  118.1 6.4 %collective-permute-done.8 = bf16[256,768]{1,0:T(8,128)(2,1)S(1)} collective-permute-done((bf16[256,768]{1,0:T(8,128)(2,1)S(1)}, bf16[256,768]{1,0:T(8,128)(2,1)S(1)}, u32[]{:S(2)}, u32[]{:S(2)}) %collective-permute-start.8) | collective-permute-done | bytes 393248 | tf_op jit(solution)/shard_map/ppermute | solution.py:335
  128.2 36.2 %all-to-all-done.2 = bf16[8,128,768]{2,1,0:T(8,128)(2,1)} async-done(((bf16[8,128,768]{2,1,0:T(8,128)(2,1)}), bf16[8,128,768]{2,1,0:T(8,128)(2,1)}, u32[]{:S(2)}, u32[]{:S(2)}) %all-to-all-start.2) | async-done | bytes 1572896 | tf_op jit(solution)/shard_map/all_to_all | solution.py:381
  164.4 25.0 %branch_rows.2 = (bf16[1024,2048]{1,0:T(8,128)(2,1)}, bf16[1024,2048]{1,0:T(8,128)(2,1)}, bf16[1024,2048]{1,0:T(8,128)(2,1)}, bf16[1024,768]{1,0:T(8,128)(2,1)S(...) custom-call(bf16[1024,768]{1,0:T(8,128)(2,1)} %bitcast.21.x_ref, bf16[1024,768]{1,0:T(8,128)(2,1)} %bitcast.19.g_ref, ...), custom_call_target="tpu_custom_call" | custom-call | flops 1000 | bytes 1000 | tf_op jit(solution)/shard_map/branch_rows/pallas_call | solution.py:149
  195.1 8.6 %branch_rows.3 = (bf16[1024,512]{1,0:T(8,128)(2,1)S(1)}, bf16[1024,512]{1,0:T(8,128)(2,1)S(1)}, bf16[1024,512]{1,0:T(8,128)(2,1)S(1)}, bf16[1024,768]{1,0:T(8,12...) custom-call(bf16[1024,768]{1,0:T(8,128)(2,1)} %pad_maximum_fusion.3.x_ref, ...), custom_call_target="tpu_custom_call" | custom-call | flops 1000 | bytes 1000 | tf_op jit(solution)/shard_map/branch_rows/pallas_call | solution.py:149
  203.7 10.9 %branch_grads.3 = bf16[2,3,768,512]{3,2,1,0:T(8,128)(2,1)} custom-call(bf16[768,1024]{1,0:T(8,128)(2,1)S(1)} %get-tuple-element.88.xt_ref, bf16[768,1024]{1,0:T(8,128)(2,1)S(1)} %get-tuple-element.89.gt_ref, bf16[1024,2048]{1,0:T(8,128)(2,1)} %get-tuple-element.87.hidden_ref, bf16[1024,2048]{1,0:T(8,128)(2,1)} %get-tuple-element.90.ggate_ref, ...), custom_call_target="tpu_custom_call" | custom-call | flops 1000 | bytes 1000 | tf_op jit(solution)/shard_map/branch_grads/pallas_call | solution.py:208
  232.6 10.3 %branch_grads.2.refs_0_ = bf16[2,3,768,512]{3,2,1,0:T(8,128)(2,1)} custom-call(bf16[768,1024]{1,0:T(8,128)(2,1)S(1)} %get-tuple-element.88.xt_ref, bf16[768,1024]{1,0:T(8,128)(2,1)S(1)} %get-tuple-element.89.gt_ref, bf16[1024,2048]{1,0:T(8,128)(2,1)} %get-tuple-element.87.hidden_ref, bf16[1024,2048]{1,0:T(8,128)(2,1)} %get-tuple-element.90.ggate_ref, ...), custom_call_target="tpu_custom_call" | custom-call | flops 1000 | bytes 1000 | tf_op jit(solution)/shard_map/branch_grads/pallas_call | solution.py:208
  242.9 5.1 %shared_grads.1 = bf16[8,3,96,512]{3,2,1,0:T(8,128)(2,1)} custom-call(bf16[768,1024]{1,0:T(8,128)(2,1)S(1)} %copy-done.11, bf16[768,1024]{1,0:T(8,128)(2,1)} %get-tuple-element.93.gt_ref, bf16[1024,512]{1,0:T(8,128)(2,1)S(1)} %get-tuple-element.94.hidden_ref, bf16[1024,512]{1,0:T(8,128)(2,1)S(1)} %get-tuple-element.95.ggate_ref, ...), custom_call_target="tpu_custom_call" | custom-call | flops 1000 | bytes 1000 | tf_op jit(solution)/shard_map/shared_grads/pallas_call | solution.py:245
  248.0 7.3 %branch_out.2 = bf16[1024,768]{1,0:T(8,128)(2,1)} custom-call(bf16[1024,2048]{1,0:T(8,128)(2,1)} %get-tuple-element.87.hidden_ref, bf16[3,768,512]{2,1,0:T(8,128)(2,1)S(1)} %copy-done.3, bf16[3,768,512]{2,1,0:T(8,128)(2,1)} %collective-permute-done.6.refs_1_, bf16[3,768,512]{2,1,0:T(8,128)(2,1)} %collective-permute-done.13.refs_2_, ...), custom_call_target="tpu_custom_call" | custom-call | flops 1000 | bytes 1000 | tf_op jit(solution)/shard_map/branch_out/pallas_call | solution.py:178
  261.0 10.0 %collective-permute-done.22 = bf16[256,768]{1,0:T(8,128)(2,1)S(1)} collective-permute-done((bf16[256,768]{1,0:T(8,128)(2,1)S(1)}, bf16[256,768]{1,0:T(8,128)(2,1)S(1)}, u32[]{:S(2)}, u32[]{:S(2)}) %collective-permute-start.22) | collective-permute-done | bytes 393248 | tf_op jit(solution)/shard_map/ppermute | solution.py:335
  272.0 5.7 %all-to-all-start.4 = ((bf16[8,128,768]{2,1,0:T(8,128)(2,1)}), bf16[8,128,768]{2,1,0:T(8,128)(2,1)}, u32[]{:S(2)}, u32[]{:S(2)}) async-start(bf16[8,128,768]{2,1,0:T(8,128)(2,1)} %bitcast.27), calls=%async_computation.4 | async-start | bytes 3145728 | tf_op jit(solution)/shard_map/all_to_all | solution.py:381
  292.3 6.8 %multiply_reduce_fusion = (f32[3,1024]{1,0:T(4,128)S(1)}, f32[3,1024,1024]{1,2,0:T(8,128)S(1)}) fusion(f32[3,1024,1024]{1,2,0:T(8,128)} %copy-done.13, f32[3,1024]{1,0:T(4,128)S(1)} %copy-done.41, bf16[1024,3,64]{0,2,1:T(8,128)(2,1)S(1)} %bitcast.156, f32[1024,3,3,64]{0,3,2,1:T(8,128)} %bitcast.154), kind=kOutput, calls=%fused_computation.1 | convolution fusion | flops 412087296 | bytes 25976832 | tf_op jit(solution)/shard_map/qhd,khd->hqk/dot_general | solution.py:101
  299.1 5.3 %multiply_convert_fusion = bf16[3,1024,1024]{1,2,0:T(8,128)(2,1)} fusion(f32[3,1024,1024]{1,2,0:T(8,128)S(1)} %get-tuple-element.198, f32[3,1024,1024]{1,2,0:T(8,128)S(1)} %bitcast.143, f32[3,1024]{1,0:T(4,128)S(1)} %get-tuple-element.197, f32[3,1024]{1,0:T(4,128)S(1)} %copy-done.41), kind=kLoop, calls=%fused_computation | loop fusion | flops 12582912 | bytes 31481856 | tf_op jit(solution)/shard_map/convert_element_type | solution.py:103
  304.4 5.2 %fusion.12 = f32[1024,3,64]{0,2,1:T(8,128)S(1)} fusion(bf16[3,1024,1024]{1,2,0:T(8,128)(2,1)} %multiply_convert_fusion, bf16[1024,3,32]{0,2,1:T(8,128)(2,1)} %copy-done.50, bf16[1024,3,32]{0,2,1:T(8,128)(2,1)} %copy-done.49), kind=kOutput, calls=%fused_computation.40 | convolution fusion | flops 403636224 | bytes 7471104 | tf_op jit(solution)/shard_map/hqk,qhd->khd/dot_general | solution.py:105
  316.7 11.7 %all-to-all-done.4 = bf16[8,128,768]{2,1,0:T(8,128)(2,1)} async-done(((bf16[8,128,768]{2,1,0:T(8,128)(2,1)}), bf16[8,128,768]{2,1,0:T(8,128)(2,1)}, u32[]{:S(2)}, u32[]{:S(2)}) %all-to-all-start.4) | async-done | bytes 1572896 | tf_op jit(solution)/shard_map/all_to_all | solution.py:381
  333.0 12.0 %all-to-all-start.5 = ((bf16[32,24,577]{2,1,0:T(8,128)(2,1)}), bf16[32,24,577]{2,1,0:T(8,128)(2,1)}, u32[]{:S(2)}, u32[]{:S(2)}) async-start(bf16[32,24,577]{2,1,0:T(8,128)(2,1)} %pad_maximum_fusion.7), calls=%async_computation.6 | async-start | bytes 1966080 | tf_op jit(solution)/shard_map/all_to_all | solution.py:595
  358.1 10.6 %adam_in.1 = (f32[6144,128]{1,0:T(8,128)}, f32[6144,128]{1,0:T(8,128)}, f32[6144,128]{1,0:T(8,128)}) custom-call(bf16[2,3,768,512]{3,2,1,0:T(8,128)(2,1)} %branch_grads.2.refs_0_, bf16[2,3,768,512]{3,2,1,0:T(8,128)(2,1)} %collective-permute-done.18.refs_1_, bf16[1,2,768,512]{3,2,1,0:T(8,128)(2,1)S(1)} %bitcast.139, f32[6144,128]{1,0:T(8,128)S(1)} %bitcast.138, ...), custom_call_target="tpu_custom_call" | custom-call | flops 1000 | bytes 1000 | tf_op jit(solution)/shard_map/adam_in/pallas_call | solution.py:289
  368.7 4.7 %collective-permute-done.30 = bf16[1,768,512]{2,1,0:T(8,128)(2,1)S(1)} collective-permute-done((bf16[1,768,512]{2,1,0:T(8,128)(2,1)}, bf16[1,768,512]{2,1,0:T(8,128)(2,1)S(1)}, u32[]{:S(2)}, u32[]{:S(2)}) %collective-permute-start.30) | collective-permute-done | bytes 786464 | tf_op jit(solution)/shard_map/ppermute | solution.py:335
  373.4 5.8 %adam_out.1 = (f32[1,512,768]{2,1,0:T(8,128)}, f32[1,512,768]{2,1,0:T(8,128)}, f32[1,512,768]{2,1,0:T(8,128)}) custom-call(bf16[2,3,768,512]{3,2,1,0:T(8,128)(2,1)} %branch_grads.2.refs_0_, bf16[2,3,768,512]{3,2,1,0:T(8,128)(2,1)} %collective-permute-done.18.refs_1_, bf16[1,1,768,512]{3,2,1,0:T(8,128)(2,1)S(1)} %bitcast.141, f32[1,512,768]{2,1,0:T(8,128)S(1)} %copy-done.7, ...), custom_call_target="tpu_custom_call" | custom-call | flops 1000 | bytes 1000 | tf_op jit(solution)/shard_map/adam_out/pallas_call | solution.py:322
  397.0 7.2 %collective-permute-start.29 = (bf16[24,768]{1,0:T(8,128)(2,1)}, bf16[24,768]{1,0:T(8,128)(2,1)S(1)}, u32[]{:S(2)}, u32[]{:S(2)}) collective-permute-start(bf16[24,768]{1,0:T(8,128)(2,1)} %reshape.491), channel_id=1, source_target_pairs={{0,0},{1,8},{2,16},{3,24},{4,1},{5,9},{6,17},{7,25},{8,2},{9,10},{... | collective-permute-start | bytes 110600 | tf_op jit(solution)/shard_map/ppermute | solution.py:607
  (366 shorter events, 170.5 us)
Async XLA Ops:
  7.2 25.6 %collective-permute-start = (bf16[256,768]{1,0:T(8,128)(2,1)}, bf16[256,768]{1,0:T(8,128)(2,1)}, u32[]{:S(2)}, u32[]{:S(2)}) collective-permute-start(bf16[256,768]{1,0:T(8,128)(2,1)} %param.26), channel_id=1, source_target_pairs={{0,2},{1,3},{2,0},{3,1},{4,6},{5,7},{6,4},{7,5},{8,10},{9,11},{10,... | collective-permute-start | bytes 1179656 | tf_op jit(solution)/shard_map/ppermute | solution.py:335
  7.3 32.3 %collective-permute-start.2 = (bf16[256,768]{1,0:T(8,128)(2,1)}, bf16[256,768]{1,0:T(8,128)(2,1)}, u32[]{:S(2)}, u32[]{:S(2)}) collective-permute-start(bf16[256,768]{1,0:T(8,128)(2,1)} %param.26), channel_id=1, source_target_pairs={{0,1},{1,0},{2,3},{3,2},{4,5},{5,4},{6,7},{7,6},{8,9},{9,8},{10,11... | collective-permute-start | bytes 1179656 | tf_op jit(solution)/shard_map/ppermute | solution.py:335
  11.4 31.3 %all-to-all-start = ((bf16[32,24,578]{2,1,0:T(8,128)(2,1)}), bf16[32,24,578]{2,1,0:T(8,128)(2,1)}, u32[]{:S(2)}, u32[]{:S(2)}) async-start(bf16[32,24,578]{2,1,0:T(8,128)(2,1)} %bitcast.148), calls=%async_computation | async-start | bytes 1966080 | tf_op jit(solution)/shard_map/all_to_all | solution.py:434
  17.9 75.7 %all-gather.3.cloned.1.call-start = ((), (), s32[]{:S(2)}) async-start(), calls=%async_computation.7 | async-start | bytes 1216512 | tf_op jit(solution)/shard_map/all_gather | solution.py:451
  23.0 70.7 %collective-permute-start.6 = (bf16[3,768,512]{2,1,0:T(8,128)(2,1)S(1)}, bf16[3,768,512]{2,1,0:T(8,128)(2,1)}, u32[]{:S(2)}, u32[]{:S(2)}) collective-permute-start(bf16[3,768,512]{2,1,0:T(8,128)(2,1)S(1)} %pad_maximum_fusion.1.refs_0_), channel_id=1, source_target_pairs={{0,2},{1,3},{2,0},{3,1},{4,6},{5,7},{6,4},{7,5},{8,10},{9,11},{10,... | collective-permute-start | bytes 7077896 | tf_op jit(solution)/shard_map/ppermute | solution.py:335
  49.9 49.2 %all-to-all-start.1 = ((bf16[8,128,768]{2,1,0:T(8,128)(2,1)}), bf16[8,128,768]{2,1,0:T(8,128)(2,1)}, u32[]{:S(2)}, u32[]{:S(2)}) async-start(bf16[8,128,768]{2,1,0:T(8,128)(2,1)} %bitcast.145), calls=%async_computation.1 | async-start | bytes 3145728 | tf_op jit(solution)/shard_map/all_to_all | solution.py:381
  54.7 140.4 %all-gather.5.cloned.1.call-start = ((), (), s32[]{:S(2)}) async-start(), calls=%async_computation.8 | async-start | bytes 2654208 | tf_op jit(solution)/shard_map/all_gather | solution.py:453
  99.0 65.4 %all-to-all-start.2 = ((bf16[8,128,768]{2,1,0:T(8,128)(2,1)}), bf16[8,128,768]{2,1,0:T(8,128)(2,1)}, u32[]{:S(2)}, u32[]{:S(2)}) async-start(bf16[8,128,768]{2,1,0:T(8,128)(2,1)} %bitcast.158), calls=%async_computation.2 | async-start | bytes 3145728 | tf_op jit(solution)/shard_map/all_to_all | solution.py:381
  105.0 59.4 %collective-permute-start.13 = (bf16[3,768,512]{2,1,0:T(8,128)(2,1)S(1)}, bf16[3,768,512]{2,1,0:T(8,128)(2,1)}, u32[]{:S(2)}, u32[]{:S(2)}) collective-permute-start(bf16[3,768,512]{2,1,0:T(8,128)(2,1)S(1)} %pad_maximum_fusion.1.refs_0_), channel_id=1, source_target_pairs={{0,1},{1,0},{2,3},{3,2},{4,5},{5,4},{6,7},{7,6},{8,9},{9,8},{10,11... | collective-permute-start | bytes 7077896 | tf_op jit(solution)/shard_map/ppermute | solution.py:335
  105.6 58.8 %collective-permute-start.14 = (bf16[3,768,512]{2,1,0:T(8,128)(2,1)}, bf16[3,768,512]{2,1,0:T(8,128)(2,1)}, u32[]{:S(2)}, u32[]{:S(2)}) collective-permute-start(bf16[3,768,512]{2,1,0:T(8,128)(2,1)} %collective-permute-done.6.refs_1_), channel_id=1, source_target_pairs={{0,1},{1,0},{2,3},{3,2},{4,5},{5,4},{6,7},{7,6},{8,9},{9,8},{10,11... | collective-permute-start | bytes 7077896 | tf_op jit(solution)/shard_map/ppermute | solution.py:335
  190.6 65.8 %all-to-all-start.3 = ((bf16[8,128,768]{2,1,0:T(8,128)(2,1)}), bf16[8,128,768]{2,1,0:T(8,128)(2,1)}, u32[]{:S(2)}, u32[]{:S(2)}) async-start(bf16[8,128,768]{2,1,0:T(8,128)(2,1)} %bitcast.140), calls=%async_computation.3 | async-start | bytes 3145728 | tf_op jit(solution)/shard_map/all_to_all | solution.py:381
  214.6 71.2 %collective-permute-start.18 = (bf16[2,3,768,512]{3,2,1,0:T(8,128)(2,1)}, bf16[2,3,768,512]{3,2,1,0:T(8,128)(2,1)}, u32[]{:S(2)}, u32[]{:S(2)}) collective-permute-start(bf16[2,3,768,512]{3,2,1,0:T(8,128)(2,1)} %branch_grads.3), channel_id=1, source_target_pairs={{0,1},{1,0},{2,3},{3,2},{4,5},{5,4},{6,7},{7,6},{8,9},{9,8},{10,11... | collective-permute-start | bytes 14155784 | tf_op jit(solution)/shard_map/ppermute | solution.py:335
  220.3 35.0 %collective-permute-start.17 = (bf16[256,768]{1,0:T(8,128)(2,1)S(1)}, bf16[256,768]{1,0:T(8,128)(2,1)S(1)}, u32[]{:S(2)}, u32[]{:S(2)}) collective-permute-start(bf16[256,768]{1,0:T(8,128)(2,1)S(1)} %get-tuple-element.160), channel_id=1, source_target_pairs={{0,3},{1,2},{2,1},{3,0},{4,7},{5,6},{6,5},{7,4},{8,11},{9,10},{10,... | collective-permute-start | bytes 1179656 | tf_op jit(solution)/shard_map/ppermute | solution.py:335
  222.5 33.9 %collective-permute-start.19 = (bf16[256,768]{1,0:T(8,128)(2,1)}, bf16[256,768]{1,0:T(8,128)(2,1)}, u32[]{:S(2)}, u32[]{:S(2)}) collective-permute-start(bf16[256,768]{1,0:T(8,128)(2,1)} %get-tuple-element.156), channel_id=1, source_target_pairs={{0,1},{1,0},{2,3},{3,2},{4,5},{5,4},{6,7},{7,6},{8,9},{9,8},{10,11... | collective-permute-start | bytes 1179656 | tf_op jit(solution)/shard_map/ppermute | solution.py:335
  226.1 30.3 %collective-permute-start.20 = (bf16[256,768]{1,0:T(8,128)(2,1)}, bf16[256,768]{1,0:T(8,128)(2,1)}, u32[]{:S(2)}, u32[]{:S(2)}) collective-permute-start(bf16[256,768]{1,0:T(8,128)(2,1)} %get-tuple-element.158), channel_id=1, source_target_pairs={{0,2},{1,3},{2,0},{3,1},{4,6},{5,7},{6,4},{7,5},{8,10},{9,11},{10,... | collective-permute-start | bytes 1179656 | tf_op jit(solution)/shard_map/ppermute | solution.py:335
  229.6 26.8 %collective-permute-start.21 = (bf16[256,768]{1,0:T(8,128)(2,1)}, bf16[256,768]{1,0:T(8,128)(2,1)}, u32[]{:S(2)}, u32[]{:S(2)}) collective-permute-start(bf16[256,768]{1,0:T(8,128)(2,1)} %get-tuple-element.157), channel_id=1, source_target_pairs={{0,3},{1,2},{2,1},{3,0},{4,7},{5,6},{6,5},{7,4},{8,11},{9,10},{10,... | collective-permute-start | bytes 1179656 | tf_op jit(solution)/shard_map/ppermute | solution.py:335
  272.0 56.4 %all-to-all-start.4 = ((bf16[8,128,768]{2,1,0:T(8,128)(2,1)}), bf16[8,128,768]{2,1,0:T(8,128)(2,1)}, u32[]{:S(2)}, u32[]{:S(2)}) async-start(bf16[8,128,768]{2,1,0:T(8,128)(2,1)} %bitcast.27), calls=%async_computation.4 | async-start | bytes 3145728 | tf_op jit(solution)/shard_map/all_to_all | solution.py:381
  277.7 113.1 %reduce-scatter.2.cloned.1.call-start = ((), (), s32[]{:S(2)}) async-start(), calls=%async_computation.9 | async-start | bytes 3022848 | tf_op jit(solution)/shard_map/reduce_scatter | solution.py:550
  291.1 37.3 %collective-permute-start.28 = (bf16[2,768,512]{2,1,0:T(8,128)(2,1)}, bf16[2,768,512]{2,1,0:T(8,128)(2,1)S(1)}, u32[]{:S(2)}, u32[]{:S(2)}) collective-permute-start(bf16[2,768,512]{2,1,0:T(8,128)(2,1)} %slice_bitcast_fusion), channel_id=1, source_target_pairs={{0,2},{1,3},{2,0},{3,1},{4,6},{5,7},{6,4},{7,5},{8,10},{9,11},{10,... | collective-permute-start | bytes 4718600 | tf_op jit(solution)/shard_map/ppermute | solution.py:335
  333.0 46.2 %all-to-all-start.5 = ((bf16[32,24,577]{2,1,0:T(8,128)(2,1)}), bf16[32,24,577]{2,1,0:T(8,128)(2,1)}, u32[]{:S(2)}, u32[]{:S(2)}) async-start(bf16[32,24,577]{2,1,0:T(8,128)(2,1)} %pad_maximum_fusion.7), calls=%async_computation.6 | async-start | bytes 1966080 | tf_op jit(solution)/shard_map/all_to_all | solution.py:595
  345.7 27.7 %collective-permute-start.30 = (bf16[1,768,512]{2,1,0:T(8,128)(2,1)}, bf16[1,768,512]{2,1,0:T(8,128)(2,1)S(1)}, u32[]{:S(2)}, u32[]{:S(2)}) collective-permute-start(bf16[1,768,512]{2,1,0:T(8,128)(2,1)} %slice_bitcast_fusion.1), channel_id=1, source_target_pairs={{0,2},{1,3},{2,0},{3,1},{4,6},{5,7},{6,4},{7,5},{8,10},{9,11},{10,... | collective-permute-start | bytes 2359304 | tf_op jit(solution)/shard_map/ppermute | solution.py:335
  350.0 40.8 %collective-permute-start.25 = (bf16[256,768]{1,0:T(8,128)(2,1)}, bf16[256,768]{1,0:T(8,128)(2,1)}, u32[]{:S(2)}, u32[]{:S(2)}) collective-permute-start(bf16[256,768]{1,0:T(8,128)(2,1)} %get-tuple-element.150), channel_id=1, source_target_pairs={{0,1},{1,0},{2,3},{3,2},{4,5},{5,4},{6,7},{7,6},{8,9},{9,8},{10,11... | collective-permute-start | bytes 1179656 | tf_op jit(solution)/shard_map/ppermute | solution.py:335
  350.4 40.4 %collective-permute-start.26 = (bf16[256,768]{1,0:T(8,128)(2,1)}, bf16[256,768]{1,0:T(8,128)(2,1)}, u32[]{:S(2)}, u32[]{:S(2)}) collective-permute-start(bf16[256,768]{1,0:T(8,128)(2,1)} %get-tuple-element.149), channel_id=1, source_target_pairs={{0,2},{1,3},{2,0},{3,1},{4,6},{5,7},{6,4},{7,5},{8,10},{9,11},{10,... | collective-permute-start | bytes 1179656 | tf_op jit(solution)/shard_map/ppermute | solution.py:335
  352.0 38.8 %collective-permute-start.27 = (bf16[256,768]{1,0:T(8,128)(2,1)}, bf16[256,768]{1,0:T(8,128)(2,1)}, u32[]{:S(2)}, u32[]{:S(2)}) collective-permute-start(bf16[256,768]{1,0:T(8,128)(2,1)} %get-tuple-element.148), channel_id=1, source_target_pairs={{0,3},{1,2},{2,1},{3,0},{4,7},{5,6},{6,5},{7,4},{8,11},{9,10},{10,... | collective-permute-start | bytes 1179656 | tf_op jit(solution)/shard_map/ppermute | solution.py:335
  (109 other events, 1159.3 us)
Sparse Core Ops, SparseCore 0:
  24.1 69.4 all-gather.2
  96.4 75.1 all-gather.4
  285.9 94.6 reduce-scatter.1
where the time goes:
time: 428 us; the launch traced here: 420 us
  waiting for transfers between devices  103 us (24%)
  Pallas kernels  85.3 us (20%)
  starting transfers between devices  70.5 us (16%)
  other arithmetic  55.8 us (13%)
  matrix products  54 us (13%)
  local copies, waits for them, and re-layouts  35.6 us (8%)
  between operations  15.6 us (4%)
    ppermute x30, waiting for transfers between devices, swap(): return lax.ppermute(value, axis, [(i, i ^ mask) for i in range(count)])  50.7 us
    all_to_all x4, waiting for transfers between devices, exchange(): lax.all_to_all(value, 'wide', split_axis=0, concat_axis=0, tiled=True)  47.9 us
    pallas_call x2, Pallas kernels, branch_rows(): pl.pallas_call(functools.partial(branch_rows_kernel, len(chunks)), grid=(...  33.7 us
    ppermute x30, starting transfers between devices, swap(): return lax.ppermute(value, axis, [(i, i ^ mask) for i in range(count)])  23.4 us
    pallas_call x2, Pallas kernels, branch_grads(): pl.pallas_call(branch_grads_kernel, grid=(chunks, width // block), in_spe...  21.2 us
    all_to_all x4, starting transfers between devices, exchange(): lax.all_to_all(value, 'wide', split_axis=0, concat_axis=0, tiled=True)  20.9 us
    unnamed x188, local copies, waits for them, and re-layouts  15.2 us
    dot_general x6, matrix products, dot(): return jnp.dot(a, b, preferred_element_type=FULL)  13.6 us
  transfers between devices with their start and end apart: 40, of which 13 were waited for; matrix products, arithmetic and copies ran while one was open for 30% of the time, Pallas kernels for 20%

commit v1 on v0

--- a/solution.py
+++ b/solution.py
@@ -431,6 +431,7 @@
     sent = jnp.broadcast_to(cut[None], (wide,) + cut.shape).reshape(
         wide * count, rows_weight, 3 * head_width + 2
     )
+    sent, mix_out_low = lax.optimization_barrier((sent, mixing_out.astype(LOW)))
     got = lax.all_to_all(sent, ("wide", "tensor"), split_axis=0, concat_axis=0, tiled=True)
     got = got.reshape(width, 3 * head_width + 2)
     w_qkv = got[:, : 3 * head_width]
@@ -448,7 +449,7 @@
     shared_low = jnp.concatenate(
         [shared_in.astype(LOW).transpose(1, 0, 2), shared_out.astype(LOW).T[None]], axis=0
     )
-    w_mix_out = lax.all_gather(mixing_out.astype(LOW), ("wide", "tensor"), axis=0, tiled=True)
+    w_mix_out = lax.all_gather(mix_out_low, ("wide", "tensor"), axis=0, tiled=True)
     shared_low = after(shared_low, w_mix_out)
     w_shared = lax.all_gather(shared_low, "wide", axis=1, tiled=True)
 
@@ -516,7 +517,7 @@
     ex_grads = functools.partial(branch_grads, (ex_xt, ex_gt), ex_states)
     if count == 4:
         ex_sent = swap(ex_grads(2, 2, ex_size), "tensor", 1, count)
-        ex_kept = ex_grads(0, 2, ex_size)
+        ex_kept = ()
     else:
         ex_sent, ex_kept = (), ex_grads(0, count, ex_size)
     out_rows = branch_out(ex_states[0], expert_chunks)
@@ -530,6 +531,9 @@
     gain_two_part = jnp.sum(grad_normed_two * hat_two, axis=0)
     grad_residual = grad_out + grad_part
     grad_res_low = grad_residual.astype(LOW)
+    if count == 4:
+        ex_states = list(after(tuple(ex_states), grad_res_low))
+        ex_kept = branch_grads((ex_xt, ex_gt), ex_states, 0, 2, ex_size)
     w_mix_pad = jnp.pad(w_mix_out, ((0, head_pad * HEAD), (0, 0)))
     grad_res_parts = gather_relative(grad_res_low, count)
     grad_res_all = jnp.concatenate(by_rank(grad_res_parts, rank), axis=0)
@@ -599,7 +603,10 @@
         concat_axis=0,
         tiled=True,
     )
-    row_grads, sums, sh_grads = after((row_grads, sums, sh_grads), got)
+    in_results = adam_in(in_parts, expert_in, expert_in_mean, expert_in_square, RATES[5])
+    out_results = adam_out(out_parts, expert_out, expert_out_mean, expert_out_square, RATES[6])
+    row_grads, in_results = lax.optimization_barrier((row_grads, in_results))
+    sums, sh_grads, out_results = lax.optimization_barrier((sums, sh_grads, out_results))
     grad_normed_one = sum(part.astype(FULL) for part in row_grads)
     if turns:
         sh_grads = sums[: 3 * rows_shared].reshape(3, rows_shared, sh_size).astype(FULL)
@@ -640,8 +647,8 @@
     results = [mixed.astype(LOW), input_grad, logit_grad]
     for number, (weight, mean, square, gradient) in enumerate(gradients):
         results.extend(adam_step(weight, mean, square, gradient, RATES[number]))
-    results.extend(adam_in(in_parts, expert_in, expert_in_mean, expert_in_square, RATES[5]))
-    results.extend(adam_out(out_parts, expert_out, expert_out_mean, expert_out_square, RATES[6]))
+    results.extend(in_results)
+    results.extend(out_results)
     return tuple(results)
 
 

time: 428 us -> 425 us (level)
  local copies, waits for them, and re-layouts: 35.6 us -> 29 us
    ppermute x30, waiting for transfers between devices: 50.7 us -> 66.5 us  [swap(): return lax.ppermute(value, axis, [(i, i ^ mask) for i in range(count)])]
    all_to_all x4, waiting for transfers between devices: 47.9 us -> 34.7 us  [exchange(): lax.all_to_all(value, 'wide', split_axis=0, concat_axis=0, tiled=True)]
    ppermute x30, starting transfers between devices: 23.4 us -> 28.7 us  [swap(): return lax.ppermute(value, axis, [(i, i ^ mask) for i in range(count)])]
    unnamed x188 -> x192, local copies, waits for them, and re-layouts: 15.2 us -> 14.3 us
  transfers between devices with their start and end apart: 40 -> 40, of which waited for: 13 -> 14; matrix products, arithmetic and copies ran while one was open for 30% -> 30% of each run, Pallas kernels for 20% -> 20%
where the time goes in v1:
time: 425 us; the launch traced here: 417 us
  waiting for transfers between devices  106 us (25%)
  Pallas kernels  83.9 us (20%)
  starting transfers between devices  73.4 us (17%)
  other arithmetic  58.1 us (14%)
  matrix products  51.4 us (12%)
  local copies, waits for them, and re-layouts  29 us (7%)
  between operations  15.7 us (4%)
    ppermute x30, waiting for transfers between devices, swap(): return lax.ppermute(value, axis, [(i, i ^ mask) for i in range(count)])  66.5 us
    all_to_all x4, waiting for transfers between devices, exchange(): lax.all_to_all(value, 'wide', split_axis=0, concat_axis=0, tiled=True)  34.7 us
    pallas_call x2, Pallas kernels, branch_rows(): pl.pallas_call(functools.partial(branch_rows_kernel, len(chunks)), grid=(...  33.7 us
    ppermute x30, starting transfers between devices, swap(): return lax.ppermute(value, axis, [(i, i ^ mask) for i in range(count)])  28.7 us
    all_to_all x4, starting transfers between devices, exchange(): lax.all_to_all(value, 'wide', split_axis=0, concat_axis=0, tiled=True)  21.6 us
    pallas_call x2, Pallas kernels, branch_grads(): pl.pallas_call(branch_grads_kernel, grid=(chunks, width // block), in_spe...  21.2 us
    unnamed x192, local copies, waits for them, and re-layouts  14.3 us
    dot_general x6, matrix products, dot(): return jnp.dot(a, b, preferred_element_type=FULL)  13.6 us
  transfers between devices with their start and end apart: 40, of which 14 were waited for; matrix products, arithmetic and copies ran while one was open for 30% of the time, Pallas kernels for 20%

profile of v1, /device:TPU:3, one launch (start us, length us, event | category | flops | bytes accessed | tf_op | source)
XLA Modules:
  0.0 417.3 jit_solution(14205841779043862577)
XLA Ops:
  12.9 6.5 %all-to-all-start = ((bf16[32,24,578]{2,1,0:T(8,128)(2,1)}), bf16[32,24,578]{2,1,0:T(8,128)(2,1)}, u32[]{:S(2)}, u32[]{:S(2)}) async-start(bf16[32,24,578]{2,1,0:T(8,128)(2,1)} %bitcast.149), calls=%async_computation | async-start | bytes 1966080 | tf_op jit(solution)/shard_map/all_to_all | solution.py:435
  51.8 5.5 %all-to-all-start.1 = ((bf16[8,128,768]{2,1,0:T(8,128)(2,1)}), bf16[8,128,768]{2,1,0:T(8,128)(2,1)}, u32[]{:S(2)}, u32[]{:S(2)}) async-start(bf16[8,128,768]{2,1,0:T(8,128)(2,1)} %bitcast.146), calls=%async_computation.1 | async-start | bytes 3145728 | tf_op jit(solution)/shard_map/all_to_all | solution.py:381
  76.2 12.3 %collective-permute-done.3 = bf16[256,192]{0,1:T(8,128)(2,1)S(1)} collective-permute-done((bf16[256,192]{0,1:T(8,128)(2,1)}, bf16[256,192]{0,1:T(8,128)(2,1)S(1)}, u32[]{:S(2)}, u32[]{:S(2)}) %collective-permute-start.3) | collective-permute-done | bytes 98336 | tf_op jit(solution)/shard_map/ppermute | solution.py:335
  101.0 5.9 %all-to-all-start.2 = ((bf16[8,128,768]{2,1,0:T(8,128)(2,1)}), bf16[8,128,768]{2,1,0:T(8,128)(2,1)}, u32[]{:S(2)}, u32[]{:S(2)}) async-start(bf16[8,128,768]{2,1,0:T(8,128)(2,1)} %bitcast.158), calls=%async_computation.2 | async-start | bytes 3145728 | tf_op jit(solution)/shard_map/all_to_all | solution.py:381
  109.8 8.2 %collective-permute-done.11 = bf16[256,768]{1,0:T(8,128)(2,1)S(1)} collective-permute-done((bf16[256,768]{1,0:T(8,128)(2,1)S(1)}, bf16[256,768]{1,0:T(8,128)(2,1)S(1)}, u32[]{:S(2)}, u32[]{:S(2)}) %collective-permute-start.11) | collective-permute-done | bytes 393248 | tf_op jit(solution)/shard_map/ppermute | solution.py:335
  120.0 6.4 %collective-permute-done.8 = bf16[256,768]{1,0:T(8,128)(2,1)S(1)} collective-permute-done((bf16[256,768]{1,0:T(8,128)(2,1)S(1)}, bf16[256,768]{1,0:T(8,128)(2,1)S(1)}, u32[]{:S(2)}, u32[]{:S(2)}) %collective-permute-start.8) | collective-permute-done | bytes 393248 | tf_op jit(solution)/shard_map/ppermute | solution.py:335
  130.2 34.7 %all-to-all-done.2 = bf16[8,128,768]{2,1,0:T(8,128)(2,1)} async-done(((bf16[8,128,768]{2,1,0:T(8,128)(2,1)}), bf16[8,128,768]{2,1,0:T(8,128)(2,1)}, u32[]{:S(2)}, u32[]{:S(2)}) %all-to-all-start.2) | async-done | bytes 1572896 | tf_op jit(solution)/shard_map/all_to_all | solution.py:381
  164.9 25.0 %branch_rows.2 = (bf16[1024,2048]{1,0:T(8,128)(2,1)}, bf16[1024,2048]{1,0:T(8,128)(2,1)}, bf16[1024,2048]{1,0:T(8,128)(2,1)}, bf16[1024,768]{1,0:T(8,128)(2,1)S(...) custom-call(bf16[1024,768]{1,0:T(8,128)(2,1)} %bitcast.21.x_ref, bf16[1024,768]{1,0:T(8,128)(2,1)} %bitcast.19.g_ref, ...), custom_call_target="tpu_custom_call" | custom-call | flops 1000 | bytes 1000 | tf_op jit(solution)/shard_map/branch_rows/pallas_call | solution.py:149
  195.5 8.6 %branch_rows.3 = (bf16[1024,512]{1,0:T(8,128)(2,1)S(1)}, bf16[1024,512]{1,0:T(8,128)(2,1)S(1)}, bf16[1024,512]{1,0:T(8,128)(2,1)S(1)}, bf16[1024,768]{1,0:T(8,12...) custom-call(bf16[1024,768]{1,0:T(8,128)(2,1)} %pad_maximum_fusion.3.x_ref, ...), custom_call_target="tpu_custom_call" | custom-call | flops 1000 | bytes 1000 | tf_op jit(solution)/shard_map/branch_rows/pallas_call | solution.py:149
  204.1 10.9 %branch_grads.3 = bf16[2,3,768,512]{3,2,1,0:T(8,128)(2,1)} custom-call(bf16[768,1024]{1,0:T(8,128)(2,1)S(1)} %get-tuple-element.106.xt_ref, bf16[768,1024]{1,0:T(8,128)(2,1)S(1)} %get-tuple-element.107.gt_ref, bf16[1024,2048]{1,0:T(8,128)(2,1)} %get-tuple-element.111.hidden_ref, bf16[1024,2048]{1,0:T(8,128)(2,1)} %get-tuple-element.112.ggate_ref, ...), custom_call_target="tpu_custom_call" | custom-call | flops 1000 | bytes 1000 | tf_op jit(solution)/shard_map/branch_grads/pallas_call | solution.py:208
  235.8 5.1 %shared_grads.1 = bf16[8,3,96,512]{3,2,1,0:T(8,128)(2,1)} custom-call(bf16[768,1024]{1,0:T(8,128)(2,1)S(1)} %copy-done.14, bf16[768,1024]{1,0:T(8,128)(2,1)} %get-tuple-element.101.gt_ref, bf16[1024,512]{1,0:T(8,128)(2,1)S(1)} %get-tuple-element.102.hidden_ref, bf16[1024,512]{1,0:T(8,128)(2,1)S(1)} %get-tuple-element.103.ggate_ref, ...), custom_call_target="tpu_custom_call" | custom-call | flops 1000 | bytes 1000 | tf_op jit(solution)/shard_map/shared_grads/pallas_call | solution.py:245
  240.8 6.3 %branch_out.2 = bf16[1024,768]{1,0:T(8,128)(2,1)S(1)} custom-call(bf16[1024,2048]{1,0:T(8,128)(2,1)} %get-tuple-element.111.hidden_ref, bf16[3,768,512]{2,1,0:T(8,128)(2,1)S(1)} %copy-done.3, bf16[3,768,512]{2,1,0:T(8,128)(2,1)} %collective-permute-done.6.refs_1_, bf16[3,768,512]{2,1,0:T(8,128)(2,1)} %collective-permute-done.13.refs_2_, ...), custom_call_target="tpu_custom_call" | custom-call | flops 1000 | bytes 1000 | tf_op jit(solution)/shard_map/branch_out/pallas_call | solution.py:178
  249.5 8.7 %collective-permute-done.20 = bf16[256,768]{1,0:T(8,128)(2,1)} collective-permute-done((bf16[256,768]{1,0:T(8,128)(2,1)}, bf16[256,768]{1,0:T(8,128)(2,1)}, u32[]{:S(2)}, u32[]{:S(2)}) %collective-permute-start.20) | collective-permute-done | bytes 393248 | tf_op jit(solution)/shard_map/ppermute | solution.py:335
  265.1 8.6 %collective-permute-done.22 = bf16[256,768]{1,0:T(8,128)(2,1)} collective-permute-done((bf16[256,768]{1,0:T(8,128)(2,1)}, bf16[256,768]{1,0:T(8,128)(2,1)}, u32[]{:S(2)}, u32[]{:S(2)}) %collective-permute-start.22) | collective-permute-done | bytes 393248 | tf_op jit(solution)/shard_map/ppermute | solution.py:335
  276.6 5.9 %all-to-all-start.4 = ((bf16[8,128,768]{2,1,0:T(8,128)(2,1)}), bf16[8,128,768]{2,1,0:T(8,128)(2,1)}, u32[]{:S(2)}, u32[]{:S(2)}) async-start(bf16[8,128,768]{2,1,0:T(8,128)(2,1)} %bitcast.139), calls=%async_computation.4 | async-start | bytes 3145728 | tf_op jit(solution)/shard_map/all_to_all | solution.py:381
  282.6 10.3 %branch_grads.2.refs_0_ = bf16[2,3,768,512]{3,2,1,0:T(8,128)(2,1)} custom-call(bf16[768,1024]{1,0:T(8,128)(2,1)S(1)} %get-tuple-element.106.xt_ref, bf16[768,1024]{1,0:T(8,128)(2,1)S(1)} %get-tuple-element.107.gt_ref, bf16[1024,2048]{1,0:T(8,128)(2,1)} %get-tuple-element.111.hidden_ref, bf16[1024,2048]{1,0:T(8,128)(2,1)} %get-tuple-element.112.ggate_ref, ...), custom_call_target="tpu_custom_call" | custom-call | flops 1000 | bytes 1000 | tf_op jit(solution)/shard_map/branch_grads/pallas_call | solution.py:208
  307.3 6.9 %multiply_reduce_fusion = (f32[3,1024]{1,0:T(4,128)S(1)}, f32[3,1024,1024]{1,2,0:T(8,128)S(1)}) fusion(f32[3,1024,1024]{1,2,0:T(8,128)} %copy-done.16, f32[3,1024]{1,0:T(4,128)S(1)} %copy-done.46, bf16[1024,3,64]{0,2,1:T(8,128)(2,1)S(1)} %bitcast.156, f32[1024,3,3,64]{0,3,2,1:T(8,128)} %bitcast.155), kind=kOutput, calls=%fused_computation.1 | convolution fusion | flops 412087296 | bytes 25976832 | tf_op jit(solution)/shard_map/qhd,khd->hqk/dot_general | solution.py:101
  314.3 5.3 %multiply_convert_fusion = bf16[3,1024,1024]{1,2,0:T(8,128)(2,1)} fusion(f32[3,1024,1024]{1,2,0:T(8,128)S(1)} %get-tuple-element.218, f32[3,1024,1024]{1,2,0:T(8,128)S(1)} %bitcast.144, f32[3,1024]{1,0:T(4,128)S(1)} %get-tuple-element.217, f32[3,1024]{1,0:T(4,128)S(1)} %copy-done.46), kind=kLoop, calls=%fused_computation | loop fusion | flops 12582912 | bytes 31481856 | tf_op jit(solution)/shard_map/convert_element_type | solution.py:103
  319.6 5.0 %fusion.12 = f32[1024,3,64]{0,2,1:T(8,128)S(1)} fusion(bf16[3,1024,1024]{1,2,0:T(8,128)(2,1)} %multiply_convert_fusion, bf16[1024,3,32]{0,2,1:T(8,128)(2,1)S(1)} %copy-done.57, bf16[1024,3,32]{0,2,1:T(8,128)(2,1)S(1)} %copy-done.55), kind=kOutput, calls=%fused_computation.40 | convolution fusion | flops 403636224 | bytes 7471104 | tf_op jit(solution)/shard_map/hqk,qhd->khd/dot_general | solution.py:105
  345.9 8.5 %all-to-all-start.5 = ((bf16[32,24,577]{2,1,0:T(8,128)(2,1)}), bf16[32,24,577]{2,1,0:T(8,128)(2,1)}, u32[]{:S(2)}, u32[]{:S(2)}) async-start(bf16[32,24,577]{2,1,0:T(8,128)(2,1)} %pad_maximum_fusion.7), calls=%async_computation.5 | async-start | bytes 1966080 | tf_op jit(solution)/shard_map/all_to_all | solution.py:599
  359.0 10.2 %adam_in.1 = (f32[6144,128]{1,0:T(8,128)}, f32[6144,128]{1,0:T(8,128)}, f32[6144,128]{1,0:T(8,128)}) custom-call(bf16[2,3,768,512]{3,2,1,0:T(8,128)(2,1)} %branch_grads.2.refs_0_, bf16[2,3,768,512]{3,2,1,0:T(8,128)(2,1)} %collective-permute-done.21.refs_1_, bf16[1,2,768,512]{3,2,1,0:T(8,128)(2,1)S(1)} %bitcast.140, f32[6144,128]{1,0:T(8,128)S(1)} %bitcast.138, ...), custom_call_target="tpu_custom_call" | custom-call | flops 1000 | bytes 1000 | tf_op jit(solution)/shard_map/adam_in/pallas_call | solution.py:289
  375.1 10.6 %collective-permute-done.29 = bf16[1,768,512]{2,1,0:T(8,128)(2,1)S(1)} collective-permute-done((bf16[1,768,512]{2,1,0:T(8,128)(2,1)S(1)}, bf16[1,768,512]{2,1,0:T(8,128)(2,1)S(1)}, u32[]{:S(2)}, u32[]{:S(2)}) %collective-permute-start.29) | collective-permute-done | bytes 786464 | tf_op jit(solution)/shard_map/ppermute | solution.py:335
  385.7 5.8 %adam_out.1 = (f32[1,512,768]{2,1,0:T(8,128)}, f32[1,512,768]{2,1,0:T(8,128)}, f32[1,512,768]{2,1,0:T(8,128)}) custom-call(bf16[2,3,768,512]{3,2,1,0:T(8,128)(2,1)} %branch_grads.2.refs_0_, bf16[2,3,768,512]{3,2,1,0:T(8,128)(2,1)} %collective-permute-done.21.refs_1_, bf16[1,1,768,512]{3,2,1,0:T(8,128)(2,1)S(1)} %bitcast.142, f32[1,512,768]{2,1,0:T(8,128)S(1)} %copy-done.7, ...), custom_call_target="tpu_custom_call" | custom-call | flops 1000 | bytes 1000 | tf_op jit(solution)/shard_map/adam_out/pallas_call | solution.py:322
  397.6 7.6 %collective-permute-start.30 = (bf16[24,768]{1,0:T(8,128)(2,1)S(1)}, bf16[24,768]{1,0:T(8,128)(2,1)S(1)}, u32[]{:S(2)}, u32[]{:S(2)}) collective-permute-start(bf16[24,768]{1,0:T(8,128)(2,1)S(1)} %reshape.500), channel_id=1, source_target_pairs={{0,0},{1,8},{2,16},{3,24},{4,1},{5,9},{6,17},{7,25},{8,2},{9,10},{... | collective-permute-start | bytes 110600 | tf_op jit(solution)/shard_map/ppermute | solution.py:614
  (369 shorter events, 172.7 us)
Async XLA Ops:
  7.2 27.5 %collective-permute-start = (bf16[256,768]{1,0:T(8,128)(2,1)}, bf16[256,768]{1,0:T(8,128)(2,1)}, u32[]{:S(2)}, u32[]{:S(2)}) collective-permute-start(bf16[256,768]{1,0:T(8,128)(2,1)} %param.26), channel_id=1, source_target_pairs={{0,2},{1,3},{2,0},{3,1},{4,6},{5,7},{6,4},{7,5},{8,10},{9,11},{10,... | collective-permute-start | bytes 1179656 | tf_op jit(solution)/shard_map/ppermute | solution.py:335
  7.3 34.1 %collective-permute-start.2 = (bf16[256,768]{1,0:T(8,128)(2,1)}, bf16[256,768]{1,0:T(8,128)(2,1)}, u32[]{:S(2)}, u32[]{:S(2)}) collective-permute-start(bf16[256,768]{1,0:T(8,128)(2,1)} %param.26), channel_id=1, source_target_pairs={{0,1},{1,0},{2,3},{3,2},{4,5},{5,4},{6,7},{7,6},{8,9},{9,8},{10,11... | collective-permute-start | bytes 1179656 | tf_op jit(solution)/shard_map/ppermute | solution.py:335
  12.9 31.7 %all-to-all-start = ((bf16[32,24,578]{2,1,0:T(8,128)(2,1)}), bf16[32,24,578]{2,1,0:T(8,128)(2,1)}, u32[]{:S(2)}, u32[]{:S(2)}) async-start(bf16[32,24,578]{2,1,0:T(8,128)(2,1)} %bitcast.149), calls=%async_computation | async-start | bytes 1966080 | tf_op jit(solution)/shard_map/all_to_all | solution.py:435
  19.4 76.2 %all-gather.3.cloned.1.call-start = ((), (), s32[]{:S(2)}) async-start(), calls=%async_computation.7 | async-start | bytes 1216512 | tf_op jit(solution)/shard_map/all_gather | solution.py:452
  24.5 71.2 %collective-permute-start.6 = (bf16[3,768,512]{2,1,0:T(8,128)(2,1)S(1)}, bf16[3,768,512]{2,1,0:T(8,128)(2,1)}, u32[]{:S(2)}, u32[]{:S(2)}) collective-permute-start(bf16[3,768,512]{2,1,0:T(8,128)(2,1)S(1)} %pad_maximum_fusion.1.refs_0_), channel_id=1, source_target_pairs={{0,2},{1,3},{2,0},{3,1},{4,6},{5,7},{6,4},{7,5},{8,10},{9,11},{10,... | collective-permute-start | bytes 7077896 | tf_op jit(solution)/shard_map/ppermute | solution.py:335
  51.8 49.3 %all-to-all-start.1 = ((bf16[8,128,768]{2,1,0:T(8,128)(2,1)}), bf16[8,128,768]{2,1,0:T(8,128)(2,1)}, u32[]{:S(2)}, u32[]{:S(2)}) async-start(bf16[8,128,768]{2,1,0:T(8,128)(2,1)} %bitcast.146), calls=%async_computation.1 | async-start | bytes 3145728 | tf_op jit(solution)/shard_map/all_to_all | solution.py:381
  57.2 138.2 %all-gather.5.cloned.1.call-start = ((), (), s32[]{:S(2)}) async-start(), calls=%async_computation.8 | async-start | bytes 2654208 | tf_op jit(solution)/shard_map/all_gather | solution.py:454
  101.0 63.8 %all-to-all-start.2 = ((bf16[8,128,768]{2,1,0:T(8,128)(2,1)}), bf16[8,128,768]{2,1,0:T(8,128)(2,1)}, u32[]{:S(2)}, u32[]{:S(2)}) async-start(bf16[8,128,768]{2,1,0:T(8,128)(2,1)} %bitcast.158), calls=%async_computation.2 | async-start | bytes 3145728 | tf_op jit(solution)/shard_map/all_to_all | solution.py:381
  107.0 57.9 %collective-permute-start.13 = (bf16[3,768,512]{2,1,0:T(8,128)(2,1)S(1)}, bf16[3,768,512]{2,1,0:T(8,128)(2,1)}, u32[]{:S(2)}, u32[]{:S(2)}) collective-permute-start(bf16[3,768,512]{2,1,0:T(8,128)(2,1)S(1)} %pad_maximum_fusion.1.refs_0_), channel_id=1, source_target_pairs={{0,1},{1,0},{2,3},{3,2},{4,5},{5,4},{6,7},{7,6},{8,9},{9,8},{10,11... | collective-permute-start | bytes 7077896 | tf_op jit(solution)/shard_map/ppermute | solution.py:335
  107.6 57.3 %collective-permute-start.14 = (bf16[3,768,512]{2,1,0:T(8,128)(2,1)}, bf16[3,768,512]{2,1,0:T(8,128)(2,1)}, u32[]{:S(2)}, u32[]{:S(2)}) collective-permute-start(bf16[3,768,512]{2,1,0:T(8,128)(2,1)} %collective-permute-done.6.refs_1_), channel_id=1, source_target_pairs={{0,1},{1,0},{2,3},{3,2},{4,5},{5,4},{6,7},{7,6},{8,9},{9,8},{10,11... | collective-permute-start | bytes 7077896 | tf_op jit(solution)/shard_map/ppermute | solution.py:335
  191.1 58.2 %all-to-all-start.3 = ((bf16[8,128,768]{2,1,0:T(8,128)(2,1)}), bf16[8,128,768]{2,1,0:T(8,128)(2,1)}, u32[]{:S(2)}, u32[]{:S(2)}) async-start(bf16[8,128,768]{2,1,0:T(8,128)(2,1)} %bitcast.141), calls=%async_computation.3 | async-start | bytes 3145728 | tf_op jit(solution)/shard_map/all_to_all | solution.py:381
  215.0 85.5 %collective-permute-start.21 = (bf16[2,3,768,512]{3,2,1,0:T(8,128)(2,1)}, bf16[2,3,768,512]{3,2,1,0:T(8,128)(2,1)}, u32[]{:S(2)}, u32[]{:S(2)}) collective-permute-start(bf16[2,3,768,512]{3,2,1,0:T(8,128)(2,1)} %branch_grads.3), channel_id=1, source_target_pairs={{0,1},{1,0},{2,3},{3,2},{4,5},{5,4},{6,7},{7,6},{8,9},{9,8},{10,11... | collective-permute-start | bytes 14155784 | tf_op jit(solution)/shard_map/ppermute | solution.py:335
  223.5 24.8 %collective-permute-start.17 = (bf16[256,768]{1,0:T(8,128)(2,1)S(1)}, bf16[256,768]{1,0:T(8,128)(2,1)S(1)}, u32[]{:S(2)}, u32[]{:S(2)}) collective-permute-start(bf16[256,768]{1,0:T(8,128)(2,1)S(1)} %get-tuple-element.180), channel_id=1, source_target_pairs={{0,3},{1,2},{2,1},{3,0},{4,7},{5,6},{6,5},{7,4},{8,11},{9,10},{10,... | collective-permute-start | bytes 1179656 | tf_op jit(solution)/shard_map/ppermute | solution.py:335
  224.9 24.5 %collective-permute-start.18 = (bf16[256,768]{1,0:T(8,128)(2,1)}, bf16[256,768]{1,0:T(8,128)(2,1)}, u32[]{:S(2)}, u32[]{:S(2)}) collective-permute-start(bf16[256,768]{1,0:T(8,128)(2,1)} %get-tuple-element.176), channel_id=1, source_target_pairs={{0,1},{1,0},{2,3},{3,2},{4,5},{5,4},{6,7},{7,6},{8,9},{9,8},{10,11... | collective-permute-start | bytes 1179656 | tf_op jit(solution)/shard_map/ppermute | solution.py:335
  232.7 25.5 %collective-permute-start.20 = (bf16[256,768]{1,0:T(8,128)(2,1)}, bf16[256,768]{1,0:T(8,128)(2,1)}, u32[]{:S(2)}, u32[]{:S(2)}) collective-permute-start(bf16[256,768]{1,0:T(8,128)(2,1)} %get-tuple-element.177), channel_id=1, source_target_pairs={{0,3},{1,2},{2,1},{3,0},{4,7},{5,6},{6,5},{7,4},{8,11},{9,10},{10,... | collective-permute-start | bytes 1179656 | tf_op jit(solution)/shard_map/ppermute | solution.py:335
  265.0 29.7 %collective-permute-start.24 = (bf16[256,768]{1,0:T(8,128)(2,1)}, bf16[256,768]{1,0:T(8,128)(2,1)}, u32[]{:S(2)}, u32[]{:S(2)}) collective-permute-start(bf16[256,768]{1,0:T(8,128)(2,1)} %fusion.89), channel_id=1, source_target_pairs={{0,1},{1,0},{2,3},{3,2},{4,5},{5,4},{6,7},{7,6},{8,9},{9,8},{10,11... | collective-permute-start | bytes 1179656 | tf_op jit(solution)/shard_map/ppermute | solution.py:335
  276.6 60.8 %all-to-all-start.4 = ((bf16[8,128,768]{2,1,0:T(8,128)(2,1)}), bf16[8,128,768]{2,1,0:T(8,128)(2,1)}, u32[]{:S(2)}, u32[]{:S(2)}) async-start(bf16[8,128,768]{2,1,0:T(8,128)(2,1)} %bitcast.139), calls=%async_computation.4 | async-start | bytes 3145728 | tf_op jit(solution)/shard_map/all_to_all | solution.py:381
  282.5 113.2 %reduce-scatter.2.cloned.1.call-start = ((), (), s32[]{:S(2)}) async-start(), calls=%async_computation.9 | async-start | bytes 3022848 | tf_op jit(solution)/shard_map/reduce_scatter | solution.py:554
  305.8 35.9 %collective-permute-start.28 = (bf16[2,768,512]{2,1,0:T(8,128)(2,1)}, bf16[2,768,512]{2,1,0:T(8,128)(2,1)S(1)}, u32[]{:S(2)}, u32[]{:S(2)}) collective-permute-start(bf16[2,768,512]{2,1,0:T(8,128)(2,1)} %slice_bitcast_fusion), channel_id=1, source_target_pairs={{0,2},{1,3},{2,0},{3,1},{4,6},{5,7},{6,4},{7,5},{8,10},{9,11},{10,... | collective-permute-start | bytes 4718600 | tf_op jit(solution)/shard_map/ppermute | solution.py:335
  333.0 36.2 %collective-permute-start.25 = (bf16[256,768]{1,0:T(8,128)(2,1)}, bf16[256,768]{1,0:T(8,128)(2,1)}, u32[]{:S(2)}, u32[]{:S(2)}) collective-permute-start(bf16[256,768]{1,0:T(8,128)(2,1)} %get-tuple-element.170), channel_id=1, source_target_pairs={{0,1},{1,0},{2,3},{3,2},{4,5},{5,4},{6,7},{7,6},{8,9},{9,8},{10,11... | collective-permute-start | bytes 1179656 | tf_op jit(solution)/shard_map/ppermute | solution.py:335
  333.6 35.7 %collective-permute-start.26 = (bf16[256,768]{1,0:T(8,128)(2,1)}, bf16[256,768]{1,0:T(8,128)(2,1)}, u32[]{:S(2)}, u32[]{:S(2)}) collective-permute-start(bf16[256,768]{1,0:T(8,128)(2,1)} %get-tuple-element.169), channel_id=1, source_target_pairs={{0,2},{1,3},{2,0},{3,1},{4,6},{5,7},{6,4},{7,5},{8,10},{9,11},{10,... | collective-permute-start | bytes 1179656 | tf_op jit(solution)/shard_map/ppermute | solution.py:335
  333.9 35.3 %collective-permute-start.27 = (bf16[256,768]{1,0:T(8,128)(2,1)}, bf16[256,768]{1,0:T(8,128)(2,1)}, u32[]{:S(2)}, u32[]{:S(2)}) collective-permute-start(bf16[256,768]{1,0:T(8,128)(2,1)} %get-tuple-element.168), channel_id=1, source_target_pairs={{0,3},{1,2},{2,1},{3,0},{4,7},{5,6},{6,5},{7,4},{8,11},{9,10},{10,... | collective-permute-start | bytes 1179656 | tf_op jit(solution)/shard_map/ppermute | solution.py:335
  345.9 45.7 %all-to-all-start.5 = ((bf16[32,24,577]{2,1,0:T(8,128)(2,1)}), bf16[32,24,577]{2,1,0:T(8,128)(2,1)}, u32[]{:S(2)}, u32[]{:S(2)}) async-start(bf16[32,24,577]{2,1,0:T(8,128)(2,1)} %pad_maximum_fusion.7), calls=%async_computation.5 | async-start | bytes 1966080 | tf_op jit(solution)/shard_map/all_to_all | solution.py:599
  358.8 26.9 %collective-permute-start.29 = (bf16[1,768,512]{2,1,0:T(8,128)(2,1)S(1)}, bf16[1,768,512]{2,1,0:T(8,128)(2,1)S(1)}, u32[]{:S(2)}, u32[]{:S(2)}) collective-permute-start(bf16[1,768,512]{2,1,0:T(8,128)(2,1)S(1)} %copy-done.47), channel_id=1, source_target_pairs={{0,2},{1,3},{2,0},{3,1},{4,6},{5,7},{6,4},{7,5},{8,10},{9,11},{10,... | collective-permute-start | bytes 2359304 | tf_op jit(solution)/shard_map/ppermute | solution.py:335
  (110 other events, 969.0 us)
Sparse Core Ops, SparseCore 0:
  24.7 70.8 all-gather.2
  98.4 75.0 all-gather.4
  300.6 88.9 reduce-scatter.1

commit v2 on v1

--- a/solution.py
+++ b/solution.py
@@ -517,7 +517,7 @@
     ex_grads = functools.partial(branch_grads, (ex_xt, ex_gt), ex_states)
     if count == 4:
         ex_sent = swap(ex_grads(2, 2, ex_size), "tensor", 1, count)
-        ex_kept = ()
+        ex_kept = ex_grads(0, 2, ex_size)
     else:
         ex_sent, ex_kept = (), ex_grads(0, count, ex_size)
     out_rows = branch_out(ex_states[0], expert_chunks)
@@ -531,9 +531,6 @@
     gain_two_part = jnp.sum(grad_normed_two * hat_two, axis=0)
     grad_residual = grad_out + grad_part
     grad_res_low = grad_residual.astype(LOW)
-    if count == 4:
-        ex_states = list(after(tuple(ex_states), grad_res_low))
-        ex_kept = branch_grads((ex_xt, ex_gt), ex_states, 0, 2, ex_size)
     w_mix_pad = jnp.pad(w_mix_out, ((0, head_pad * HEAD), (0, 0)))
     grad_res_parts = gather_relative(grad_res_low, count)
     grad_res_all = jnp.concatenate(by_rank(grad_res_parts, rank), axis=0)

time: 425 us -> 414 us (0.974)
  waiting for transfers between devices: 106 us -> 94 us
    ppermute x30, waiting for transfers between devices: 66.5 us -> 51.3 us  [swap(): return lax.ppermute(value, axis, [(i, i ^ mask) for i in range(count)])]
    all_to_all x1, starting transfers between devices: 8.5 us -> 13.9 us  [body(): lax.all_to_all(sent.reshape(wide * count, rows_weight, 3 * head_width + 1...]
    unnamed x192 -> x204, local copies, waits for them, and re-layouts: 14.3 us -> 14.1 us
  transfers between devices with their start and end apart: 40 -> 40, of which waited for: 14 -> 12; matrix products, arithmetic and copies ran while one was open for 30% -> 30% of each run, Pallas kernels for 20% -> 21%
where the time goes in v2:
time: 414 us; the launch traced here: 406 us
  waiting for transfers between devices  94 us (23%)
  Pallas kernels  85 us (21%)
  starting transfers between devices  76.1 us (18%)
  other arithmetic  54.8 us (13%)
  matrix products  52.1 us (13%)
  local copies, waits for them, and re-layouts  28.1 us (7%)
  between operations  15.8 us (4%)
    ppermute x30, waiting for transfers between devices, swap(): return lax.ppermute(value, axis, [(i, i ^ mask) for i in range(count)])  51.3 us
    all_to_all x4, waiting for transfers between devices, exchange(): lax.all_to_all(value, 'wide', split_axis=0, concat_axis=0, tiled=True)  38.3 us
    pallas_call x2, Pallas kernels, branch_rows(): pl.pallas_call(functools.partial(branch_rows_kernel, len(chunks)), grid=(...  33.7 us
    ppermute x30, starting transfers between devices, swap(): return lax.ppermute(value, axis, [(i, i ^ mask) for i in range(count)])  27 us
    all_to_all x4, starting transfers between devices, exchange(): lax.all_to_all(value, 'wide', split_axis=0, concat_axis=0, tiled=True)  22.1 us
    pallas_call x2, Pallas kernels, branch_grads(): pl.pallas_call(branch_grads_kernel, grid=(chunks, width // block), in_spe...  21.3 us
    unnamed x204, local copies, waits for them, and re-layouts  14.1 us
    all_to_all x1, starting transfers between devices, body(): lax.all_to_all(sent.reshape(wide * count, rows_weight, 3 * head_width + 1...  13.9 us
  transfers between devices with their start and end apart: 40, of which 12 were waited for; matrix products, arithmetic and copies ran while one was open for 30% of the time, Pallas kernels for 21%

profile of v2, /device:TPU:3, one launch (start us, length us, event | category | flops | bytes accessed | tf_op | source)
XLA Modules:
  0.0 406.0 jit_solution(3350718382271052111)
XLA Ops:
  12.9 6.5 %all-to-all-start = ((bf16[32,24,578]{2,1,0:T(8,128)(2,1)}), bf16[32,24,578]{2,1,0:T(8,128)(2,1)}, u32[]{:S(2)}, u32[]{:S(2)}) async-start(bf16[32,24,578]{2,1,0:T(8,128)(2,1)} %bitcast.148), calls=%async_computation | async-start | bytes 1966080 | tf_op jit(solution)/shard_map/all_to_all | solution.py:435
  51.7 5.5 %all-to-all-start.1 = ((bf16[8,128,768]{2,1,0:T(8,128)(2,1)}), bf16[8,128,768]{2,1,0:T(8,128)(2,1)}, u32[]{:S(2)}, u32[]{:S(2)}) async-start(bf16[8,128,768]{2,1,0:T(8,128)(2,1)} %bitcast.145), calls=%async_computation.1 | async-start | bytes 3145728 | tf_op jit(solution)/shard_map/all_to_all | solution.py:381
  76.2 12.3 %collective-permute-done.3 = bf16[256,192]{0,1:T(8,128)(2,1)S(1)} collective-permute-done((bf16[256,192]{0,1:T(8,128)(2,1)}, bf16[256,192]{0,1:T(8,128)(2,1)S(1)}, u32[]{:S(2)}, u32[]{:S(2)}) %collective-permute-start.3) | collective-permute-done | bytes 98336 | tf_op jit(solution)/shard_map/ppermute | solution.py:335
  101.0 5.7 %all-to-all-start.2 = ((bf16[8,128,768]{2,1,0:T(8,128)(2,1)}), bf16[8,128,768]{2,1,0:T(8,128)(2,1)}, u32[]{:S(2)}, u32[]{:S(2)}) async-start(bf16[8,128,768]{2,1,0:T(8,128)(2,1)} %bitcast.157), calls=%async_computation.2 | async-start | bytes 3145728 | tf_op jit(solution)/shard_map/all_to_all | solution.py:381
  109.6 8.2 %collective-permute-done.11 = bf16[256,768]{1,0:T(8,128)(2,1)S(1)} collective-permute-done((bf16[256,768]{1,0:T(8,128)(2,1)S(1)}, bf16[256,768]{1,0:T(8,128)(2,1)S(1)}, u32[]{:S(2)}, u32[]{:S(2)}) %collective-permute-start.11) | collective-permute-done | bytes 393248 | tf_op jit(solution)/shard_map/ppermute | solution.py:335
  119.8 6.4 %collective-permute-done.8 = bf16[256,768]{1,0:T(8,128)(2,1)S(1)} collective-permute-done((bf16[256,768]{1,0:T(8,128)(2,1)S(1)}, bf16[256,768]{1,0:T(8,128)(2,1)S(1)}, u32[]{:S(2)}, u32[]{:S(2)}) %collective-permute-start.8) | collective-permute-done | bytes 393248 | tf_op jit(solution)/shard_map/ppermute | solution.py:335
  130.0 34.1 %all-to-all-done.2 = bf16[8,128,768]{2,1,0:T(8,128)(2,1)} async-done(((bf16[8,128,768]{2,1,0:T(8,128)(2,1)}), bf16[8,128,768]{2,1,0:T(8,128)(2,1)}, u32[]{:S(2)}, u32[]{:S(2)}) %all-to-all-start.2) | async-done | bytes 1572896 | tf_op jit(solution)/shard_map/all_to_all | solution.py:381
  164.1 25.1 %branch_rows.2 = (bf16[1024,2048]{1,0:T(8,128)(2,1)}, bf16[1024,2048]{1,0:T(8,128)(2,1)}, bf16[1024,2048]{1,0:T(8,128)(2,1)}, bf16[1024,768]{1,0:T(8,128)(2,1)S(...) custom-call(bf16[1024,768]{1,0:T(8,128)(2,1)} %bitcast.21.x_ref, bf16[1024,768]{1,0:T(8,128)(2,1)} %bitcast.19.g_ref, ...), custom_call_target="tpu_custom_call" | custom-call | flops 1000 | bytes 1000 | tf_op jit(solution)/shard_map/branch_rows/pallas_call | solution.py:149
  190.3 5.2 %all-to-all-start.3 = ((bf16[8,128,768]{2,1,0:T(8,128)(2,1)}), bf16[8,128,768]{2,1,0:T(8,128)(2,1)}, u32[]{:S(2)}, u32[]{:S(2)}) async-start(bf16[8,128,768]{2,1,0:T(8,128)(2,1)} %bitcast.140), calls=%async_computation.3 | async-start | bytes 3145728 | tf_op jit(solution)/shard_map/all_to_all | solution.py:381
  195.5 8.6 %branch_rows.3 = (bf16[1024,512]{1,0:T(8,128)(2,1)S(1)}, bf16[1024,512]{1,0:T(8,128)(2,1)S(1)}, bf16[1024,512]{1,0:T(8,128)(2,1)S(1)}, bf16[1024,768]{1,0:T(8,12...) custom-call(bf16[1024,768]{1,0:T(8,128)(2,1)} %pad_maximum_fusion.3.x_ref, ...), custom_call_target="tpu_custom_call" | custom-call | flops 1000 | bytes 1000 | tf_op jit(solution)/shard_map/branch_rows/pallas_call | solution.py:149
  204.2 10.9 %branch_grads.3 = bf16[2,3,768,512]{3,2,1,0:T(8,128)(2,1)} custom-call(bf16[768,1024]{1,0:T(8,128)(2,1)S(1)} %get-tuple-element.98.xt_ref, bf16[768,1024]{1,0:T(8,128)(2,1)S(1)} %get-tuple-element.99.gt_ref, bf16[1024,2048]{1,0:T(8,128)(2,1)} %get-tuple-element.97.hidden_ref, bf16[1024,2048]{1,0:T(8,128)(2,1)} %get-tuple-element.100.ggate_ref, ...), custom_call_target="tpu_custom_call" | custom-call | flops 1000 | bytes 1000 | tf_op jit(solution)/shard_map/branch_grads/pallas_call | solution.py:208
  236.0 10.4 %branch_grads.2.refs_0_ = bf16[2,3,768,512]{3,2,1,0:T(8,128)(2,1)} custom-call(bf16[768,1024]{1,0:T(8,128)(2,1)S(1)} %get-tuple-element.98.xt_ref, bf16[768,1024]{1,0:T(8,128)(2,1)S(1)} %get-tuple-element.99.gt_ref, bf16[1024,2048]{1,0:T(8,128)(2,1)} %get-tuple-element.97.hidden_ref, bf16[1024,2048]{1,0:T(8,128)(2,1)} %get-tuple-element.100.ggate_ref, ...), custom_call_target="tpu_custom_call" | custom-call | flops 1000 | bytes 1000 | tf_op jit(solution)/shard_map/branch_grads/pallas_call | solution.py:208
  246.4 5.1 %shared_grads.1 = bf16[8,3,96,512]{3,2,1,0:T(8,128)(2,1)} custom-call(bf16[768,1024]{1,0:T(8,128)(2,1)S(1)} %copy-done.13, bf16[768,1024]{1,0:T(8,128)(2,1)} %get-tuple-element.103.gt_ref, bf16[1024,512]{1,0:T(8,128)(2,1)S(1)} %get-tuple-element.104.hidden_ref, bf16[1024,512]{1,0:T(8,128)(2,1)S(1)} %get-tuple-element.105.ggate_ref, ...), custom_call_target="tpu_custom_call" | custom-call | flops 1000 | bytes 1000 | tf_op jit(solution)/shard_map/shared_grads/pallas_call | solution.py:245
  251.5 7.3 %branch_out.2 = bf16[1024,768]{1,0:T(8,128)(2,1)} custom-call(bf16[1024,2048]{1,0:T(8,128)(2,1)} %get-tuple-element.97.hidden_ref, bf16[3,768,512]{2,1,0:T(8,128)(2,1)S(1)} %copy-done.3, bf16[3,768,512]{2,1,0:T(8,128)(2,1)} %collective-permute-done.6.refs_1_, bf16[3,768,512]{2,1,0:T(8,128)(2,1)} %collective-permute-done.13.refs_2_, ...), custom_call_target="tpu_custom_call" | custom-call | flops 1000 | bytes 1000 | tf_op jit(solution)/shard_map/branch_out/pallas_call | solution.py:178
  264.4 8.7 %collective-permute-done.22 = bf16[256,768]{1,0:T(8,128)(2,1)S(1)} collective-permute-done((bf16[256,768]{1,0:T(8,128)(2,1)S(1)}, bf16[256,768]{1,0:T(8,128)(2,1)S(1)}, u32[]{:S(2)}, u32[]{:S(2)}) %collective-permute-start.22) | collective-permute-done | bytes 393248 | tf_op jit(solution)/shard_map/ppermute | solution.py:335
  273.7 5.7 %all-to-all-start.4 = ((bf16[8,128,768]{2,1,0:T(8,128)(2,1)}), bf16[8,128,768]{2,1,0:T(8,128)(2,1)}, u32[]{:S(2)}, u32[]{:S(2)}) async-start(bf16[8,128,768]{2,1,0:T(8,128)(2,1)} %bitcast.27), calls=%async_computation.4 | async-start | bytes 3145728 | tf_op jit(solution)/shard_map/all_to_all | solution.py:381
  294.3 7.1 %multiply_reduce_fusion = (f32[3,1024]{1,0:T(4,128)S(1)}, f32[3,1024,1024]{1,2,0:T(8,128)S(1)}) fusion(f32[3,1024,1024]{1,2,0:T(8,128)} %copy-done.15, f32[3,1024]{1,0:T(4,128)S(1)} %log_add_fusion, bf16[1024,3,64]{0,2,1:T(8,128)(2,1)S(1)} %bitcast.155, f32[1024,3,3,64]{0,3,2,1:T(8,128)} %bitcast.154), kind=kOutput, calls=%fused_computation.1 | convolution fusion | flops 412087296 | bytes 25976832 | tf_op jit(solution)/shard_map/qhd,khd->hqk/dot_general | solution.py:101
  301.4 5.3 %multiply_convert_fusion = bf16[3,1024,1024]{1,2,0:T(8,128)(2,1)} fusion(f32[3,1024,1024]{1,2,0:T(8,128)S(1)} %get-tuple-element.214, f32[3,1024,1024]{1,2,0:T(8,128)S(1)} %bitcast.143, f32[3,1024]{1,0:T(4,128)S(1)} %get-tuple-element.213, f32[3,1024]{1,0:T(4,128)S(1)} %log_add_fusion), kind=kLoop, calls=%fused_computation | loop fusion | flops 12582912 | bytes 31481856 | tf_op jit(solution)/shard_map/convert_element_type | solution.py:103
  306.7 5.0 %fusion.12 = f32[1024,3,64]{0,2,1:T(8,128)S(1)} fusion(bf16[3,1024,1024]{1,2,0:T(8,128)(2,1)} %multiply_convert_fusion, bf16[1024,3,32]{0,2,1:T(8,128)(2,1)S(1)} %copy-done.57, bf16[1024,3,32]{0,2,1:T(8,128)(2,1)S(1)} %copy-done.55), kind=kOutput, calls=%fused_computation.40 | convolution fusion | flops 403636224 | bytes 7471104 | tf_op jit(solution)/shard_map/hqk,qhd->khd/dot_general | solution.py:105
  332.8 13.9 %all-to-all-start.5 = ((bf16[32,24,577]{2,1,0:T(8,128)(2,1)}), bf16[32,24,577]{2,1,0:T(8,128)(2,1)}, u32[]{:S(2)}, u32[]{:S(2)}) async-start(bf16[32,24,577]{2,1,0:T(8,128)(2,1)} %pad_maximum_fusion.7), calls=%async_computation.5 | async-start | bytes 1966080 | tf_op jit(solution)/shard_map/all_to_all | solution.py:596
  351.4 10.2 %adam_in.1 = (f32[6144,128]{1,0:T(8,128)}, f32[6144,128]{1,0:T(8,128)}, f32[6144,128]{1,0:T(8,128)}) custom-call(bf16[2,3,768,512]{3,2,1,0:T(8,128)(2,1)} %branch_grads.2.refs_0_, bf16[2,3,768,512]{3,2,1,0:T(8,128)(2,1)} %collective-permute-done.18.refs_1_, bf16[1,2,768,512]{3,2,1,0:T(8,128)(2,1)S(1)} %bitcast.139, f32[6144,128]{1,0:T(8,128)S(1)} %bitcast.138, ...), custom_call_target="tpu_custom_call" | custom-call | flops 1000 | bytes 1000 | tf_op jit(solution)/shard_map/adam_in/pallas_call | solution.py:289
  367.4 8.5 %collective-permute-done.29 = bf16[1,768,512]{2,1,0:T(8,128)(2,1)S(1)} collective-permute-done((bf16[1,768,512]{2,1,0:T(8,128)(2,1)S(1)}, bf16[1,768,512]{2,1,0:T(8,128)(2,1)S(1)}, u32[]{:S(2)}, u32[]{:S(2)}) %collective-permute-start.29) | collective-permute-done | bytes 786464 | tf_op jit(solution)/shard_map/ppermute | solution.py:335
  375.9 5.8 %adam_out.1 = (f32[1,512,768]{2,1,0:T(8,128)}, f32[1,512,768]{2,1,0:T(8,128)}, f32[1,512,768]{2,1,0:T(8,128)}) custom-call(bf16[2,3,768,512]{3,2,1,0:T(8,128)(2,1)} %branch_grads.2.refs_0_, bf16[2,3,768,512]{3,2,1,0:T(8,128)(2,1)} %collective-permute-done.18.refs_1_, bf16[1,1,768,512]{3,2,1,0:T(8,128)(2,1)S(1)} %bitcast.141, f32[1,512,768]{2,1,0:T(8,128)S(1)} %copy-done.7, ...), custom_call_target="tpu_custom_call" | custom-call | flops 1000 | bytes 1000 | tf_op jit(solution)/shard_map/adam_out/pallas_call | solution.py:322
  387.9 6.0 %collective-permute-start.30 = (bf16[24,768]{1,0:T(8,128)(2,1)S(1)}, bf16[24,768]{1,0:T(8,128)(2,1)S(1)}, u32[]{:S(2)}, u32[]{:S(2)}) collective-permute-start(bf16[24,768]{1,0:T(8,128)(2,1)S(1)} %reshape.500), channel_id=1, source_target_pairs={{0,0},{1,8},{2,16},{3,24},{4,1},{5,9},{6,17},{7,25},{8,2},{9,10},{... | collective-permute-start | bytes 110600 | tf_op jit(solution)/shard_map/ppermute | solution.py:611
  (381 shorter events, 162.7 us)
Async XLA Ops:
  7.2 27.5 %collective-permute-start = (bf16[256,768]{1,0:T(8,128)(2,1)}, bf16[256,768]{1,0:T(8,128)(2,1)}, u32[]{:S(2)}, u32[]{:S(2)}) collective-permute-start(bf16[256,768]{1,0:T(8,128)(2,1)} %param.26), channel_id=1, source_target_pairs={{0,2},{1,3},{2,0},{3,1},{4,6},{5,7},{6,4},{7,5},{8,10},{9,11},{10,... | collective-permute-start | bytes 1179656 | tf_op jit(solution)/shard_map/ppermute | solution.py:335
  7.3 34.1 %collective-permute-start.2 = (bf16[256,768]{1,0:T(8,128)(2,1)}, bf16[256,768]{1,0:T(8,128)(2,1)}, u32[]{:S(2)}, u32[]{:S(2)}) collective-permute-start(bf16[256,768]{1,0:T(8,128)(2,1)} %param.26), channel_id=1, source_target_pairs={{0,1},{1,0},{2,3},{3,2},{4,5},{5,4},{6,7},{7,6},{8,9},{9,8},{10,11... | collective-permute-start | bytes 1179656 | tf_op jit(solution)/shard_map/ppermute | solution.py:335
  12.9 31.7 %all-to-all-start = ((bf16[32,24,578]{2,1,0:T(8,128)(2,1)}), bf16[32,24,578]{2,1,0:T(8,128)(2,1)}, u32[]{:S(2)}, u32[]{:S(2)}) async-start(bf16[32,24,578]{2,1,0:T(8,128)(2,1)} %bitcast.148), calls=%async_computation | async-start | bytes 1966080 | tf_op jit(solution)/shard_map/all_to_all | solution.py:435
  19.4 76.2 %all-gather.3.cloned.1.call-start = ((), (), s32[]{:S(2)}) async-start(), calls=%async_computation.7 | async-start | bytes 1216512 | tf_op jit(solution)/shard_map/all_gather | solution.py:452
  24.5 71.2 %collective-permute-start.6 = (bf16[3,768,512]{2,1,0:T(8,128)(2,1)S(1)}, bf16[3,768,512]{2,1,0:T(8,128)(2,1)}, u32[]{:S(2)}, u32[]{:S(2)}) collective-permute-start(bf16[3,768,512]{2,1,0:T(8,128)(2,1)S(1)} %pad_maximum_fusion.1.refs_0_), channel_id=1, source_target_pairs={{0,2},{1,3},{2,0},{3,1},{4,6},{5,7},{6,4},{7,5},{8,10},{9,11},{10,... | collective-permute-start | bytes 7077896 | tf_op jit(solution)/shard_map/ppermute | solution.py:335
  51.7 49.3 %all-to-all-start.1 = ((bf16[8,128,768]{2,1,0:T(8,128)(2,1)}), bf16[8,128,768]{2,1,0:T(8,128)(2,1)}, u32[]{:S(2)}, u32[]{:S(2)}) async-start(bf16[8,128,768]{2,1,0:T(8,128)(2,1)} %bitcast.145), calls=%async_computation.1 | async-start | bytes 3145728 | tf_op jit(solution)/shard_map/all_to_all | solution.py:381
  57.2 138.3 %all-gather.5.cloned.1.call-start = ((), (), s32[]{:S(2)}) async-start(), calls=%async_computation.8 | async-start | bytes 2654208 | tf_op jit(solution)/shard_map/all_gather | solution.py:454
  101.0 63.0 %all-to-all-start.2 = ((bf16[8,128,768]{2,1,0:T(8,128)(2,1)}), bf16[8,128,768]{2,1,0:T(8,128)(2,1)}, u32[]{:S(2)}, u32[]{:S(2)}) async-start(bf16[8,128,768]{2,1,0:T(8,128)(2,1)} %bitcast.157), calls=%async_computation.2 | async-start | bytes 3145728 | tf_op jit(solution)/shard_map/all_to_all | solution.py:381
  106.8 57.3 %collective-permute-start.13 = (bf16[3,768,512]{2,1,0:T(8,128)(2,1)S(1)}, bf16[3,768,512]{2,1,0:T(8,128)(2,1)}, u32[]{:S(2)}, u32[]{:S(2)}) collective-permute-start(bf16[3,768,512]{2,1,0:T(8,128)(2,1)S(1)} %pad_maximum_fusion.1.refs_0_), channel_id=1, source_target_pairs={{0,1},{1,0},{2,3},{3,2},{4,5},{5,4},{6,7},{7,6},{8,9},{9,8},{10,11... | collective-permute-start | bytes 7077896 | tf_op jit(solution)/shard_map/ppermute | solution.py:335
  107.3 56.7 %collective-permute-start.14 = (bf16[3,768,512]{2,1,0:T(8,128)(2,1)}, bf16[3,768,512]{2,1,0:T(8,128)(2,1)}, u32[]{:S(2)}, u32[]{:S(2)}) collective-permute-start(bf16[3,768,512]{2,1,0:T(8,128)(2,1)} %collective-permute-done.6.refs_1_), channel_id=1, source_target_pairs={{0,1},{1,0},{2,3},{3,2},{4,5},{5,4},{6,7},{7,6},{8,9},{9,8},{10,11... | collective-permute-start | bytes 7077896 | tf_op jit(solution)/shard_map/ppermute | solution.py:335
  190.3 69.5 %all-to-all-start.3 = ((bf16[8,128,768]{2,1,0:T(8,128)(2,1)}), bf16[8,128,768]{2,1,0:T(8,128)(2,1)}, u32[]{:S(2)}, u32[]{:S(2)}) async-start(bf16[8,128,768]{2,1,0:T(8,128)(2,1)} %bitcast.140), calls=%async_computation.3 | async-start | bytes 3145728 | tf_op jit(solution)/shard_map/all_to_all | solution.py:381
  215.1 72.3 %collective-permute-start.18 = (bf16[2,3,768,512]{3,2,1,0:T(8,128)(2,1)}, bf16[2,3,768,512]{3,2,1,0:T(8,128)(2,1)}, u32[]{:S(2)}, u32[]{:S(2)}) collective-permute-start(bf16[2,3,768,512]{3,2,1,0:T(8,128)(2,1)} %branch_grads.3), channel_id=1, source_target_pairs={{0,1},{1,0},{2,3},{3,2},{4,5},{5,4},{6,7},{7,6},{8,9},{9,8},{10,11... | collective-permute-start | bytes 14155784 | tf_op jit(solution)/shard_map/ppermute | solution.py:335
  223.7 35.1 %collective-permute-start.17 = (bf16[256,768]{1,0:T(8,128)(2,1)S(1)}, bf16[256,768]{1,0:T(8,128)(2,1)S(1)}, u32[]{:S(2)}, u32[]{:S(2)}) collective-permute-start(bf16[256,768]{1,0:T(8,128)(2,1)S(1)} %get-tuple-element.176), channel_id=1, source_target_pairs={{0,3},{1,2},{2,1},{3,0},{4,7},{5,6},{6,5},{7,4},{8,11},{9,10},{10,... | collective-permute-start | bytes 1179656 | tf_op jit(solution)/shard_map/ppermute | solution.py:335
  225.1 34.7 %collective-permute-start.19 = (bf16[256,768]{1,0:T(8,128)(2,1)}, bf16[256,768]{1,0:T(8,128)(2,1)}, u32[]{:S(2)}, u32[]{:S(2)}) collective-permute-start(bf16[256,768]{1,0:T(8,128)(2,1)} %get-tuple-element.172), channel_id=1, source_target_pairs={{0,1},{1,0},{2,3},{3,2},{4,5},{5,4},{6,7},{7,6},{8,9},{9,8},{10,11... | collective-permute-start | bytes 1179656 | tf_op jit(solution)/shard_map/ppermute | solution.py:335
  228.5 31.4 %collective-permute-start.20 = (bf16[256,768]{1,0:T(8,128)(2,1)}, bf16[256,768]{1,0:T(8,128)(2,1)}, u32[]{:S(2)}, u32[]{:S(2)}) collective-permute-start(bf16[256,768]{1,0:T(8,128)(2,1)} %get-tuple-element.174), channel_id=1, source_target_pairs={{0,2},{1,3},{2,0},{3,1},{4,6},{5,7},{6,4},{7,5},{8,10},{9,11},{10,... | collective-permute-start | bytes 1179656 | tf_op jit(solution)/shard_map/ppermute | solution.py:335
  232.9 26.9 %collective-permute-start.21 = (bf16[256,768]{1,0:T(8,128)(2,1)}, bf16[256,768]{1,0:T(8,128)(2,1)}, u32[]{:S(2)}, u32[]{:S(2)}) collective-permute-start(bf16[256,768]{1,0:T(8,128)(2,1)} %get-tuple-element.173), channel_id=1, source_target_pairs={{0,3},{1,2},{2,1},{3,0},{4,7},{5,6},{6,5},{7,4},{8,11},{9,10},{10,... | collective-permute-start | bytes 1179656 | tf_op jit(solution)/shard_map/ppermute | solution.py:335
  273.7 55.0 %all-to-all-start.4 = ((bf16[8,128,768]{2,1,0:T(8,128)(2,1)}), bf16[8,128,768]{2,1,0:T(8,128)(2,1)}, u32[]{:S(2)}, u32[]{:S(2)}) async-start(bf16[8,128,768]{2,1,0:T(8,128)(2,1)} %bitcast.27), calls=%async_computation.4 | async-start | bytes 3145728 | tf_op jit(solution)/shard_map/all_to_all | solution.py:381
  279.4 106.6 %reduce-scatter.2.cloned.1.call-start = ((), (), s32[]{:S(2)}) async-start(), calls=%async_computation.9 | async-start | bytes 3022848 | tf_op jit(solution)/shard_map/reduce_scatter | solution.py:551
  292.7 36.0 %collective-permute-start.28 = (bf16[2,768,512]{2,1,0:T(8,128)(2,1)}, bf16[2,768,512]{2,1,0:T(8,128)(2,1)S(1)}, u32[]{:S(2)}, u32[]{:S(2)}) collective-permute-start(bf16[2,768,512]{2,1,0:T(8,128)(2,1)} %slice_bitcast_fusion), channel_id=1, source_target_pairs={{0,2},{1,3},{2,0},{3,1},{4,6},{5,7},{6,4},{7,5},{8,10},{9,11},{10,... | collective-permute-start | bytes 4718600 | tf_op jit(solution)/shard_map/ppermute | solution.py:335
  320.0 41.6 %collective-permute-start.25 = (bf16[256,768]{1,0:T(8,128)(2,1)}, bf16[256,768]{1,0:T(8,128)(2,1)}, u32[]{:S(2)}, u32[]{:S(2)}) collective-permute-start(bf16[256,768]{1,0:T(8,128)(2,1)} %get-tuple-element.166), channel_id=1, source_target_pairs={{0,1},{1,0},{2,3},{3,2},{4,5},{5,4},{6,7},{7,6},{8,9},{9,8},{10,11... | collective-permute-start | bytes 1179656 | tf_op jit(solution)/shard_map/ppermute | solution.py:335
  320.6 41.0 %collective-permute-start.26 = (bf16[256,768]{1,0:T(8,128)(2,1)}, bf16[256,768]{1,0:T(8,128)(2,1)}, u32[]{:S(2)}, u32[]{:S(2)}) collective-permute-start(bf16[256,768]{1,0:T(8,128)(2,1)} %get-tuple-element.165), channel_id=1, source_target_pairs={{0,2},{1,3},{2,0},{3,1},{4,6},{5,7},{6,4},{7,5},{8,10},{9,11},{10,... | collective-permute-start | bytes 1179656 | tf_op jit(solution)/shard_map/ppermute | solution.py:335
  320.8 40.8 %collective-permute-start.27 = (bf16[256,768]{1,0:T(8,128)(2,1)}, bf16[256,768]{1,0:T(8,128)(2,1)}, u32[]{:S(2)}, u32[]{:S(2)}) collective-permute-start(bf16[256,768]{1,0:T(8,128)(2,1)} %get-tuple-element.164), channel_id=1, source_target_pairs={{0,3},{1,2},{2,1},{3,0},{4,7},{5,6},{6,5},{7,4},{8,11},{9,10},{10,... | collective-permute-start | bytes 1179656 | tf_op jit(solution)/shard_map/ppermute | solution.py:335
  332.8 49.1 %all-to-all-start.5 = ((bf16[32,24,577]{2,1,0:T(8,128)(2,1)}), bf16[32,24,577]{2,1,0:T(8,128)(2,1)}, u32[]{:S(2)}, u32[]{:S(2)}) async-start(bf16[32,24,577]{2,1,0:T(8,128)(2,1)} %pad_maximum_fusion.7), calls=%async_computation.5 | async-start | bytes 1966080 | tf_op jit(solution)/shard_map/all_to_all | solution.py:596
  351.1 24.8 %collective-permute-start.29 = (bf16[1,768,512]{2,1,0:T(8,128)(2,1)S(1)}, bf16[1,768,512]{2,1,0:T(8,128)(2,1)S(1)}, u32[]{:S(2)}, u32[]{:S(2)}) collective-permute-start(bf16[1,768,512]{2,1,0:T(8,128)(2,1)S(1)} %copy-done.47), channel_id=1, source_target_pairs={{0,2},{1,3},{2,0},{3,1},{4,6},{5,7},{6,4},{7,5},{8,10},{9,11},{10,... | collective-permute-start | bytes 2359304 | tf_op jit(solution)/shard_map/ppermute | solution.py:335
  (116 other events, 1004.3 us)
Sparse Core Ops, SparseCore 0:
  24.7 70.8 all-gather.2
  98.4 74.9 all-gather.4
  287.5 94.8 reduce-scatter.1

commit v3 on v2

--- a/solution.py
+++ b/solution.py
@@ -431,7 +431,8 @@
     sent = jnp.broadcast_to(cut[None], (wide,) + cut.shape).reshape(
         wide * count, rows_weight, 3 * head_width + 2
     )
-    sent, mix_out_low = lax.optimization_barrier((sent, mixing_out.astype(LOW)))
+    mix_out_low = lax.optimization_barrier(mixing_out.astype(LOW))
+    sent = after(sent, mix_out_low)
     got = lax.all_to_all(sent, ("wide", "tensor"), split_axis=0, concat_axis=0, tiled=True)
     got = got.reshape(width, 3 * head_width + 2)
     w_qkv = got[:, : 3 * head_width]

time: 414 us -> 408 us (0.986)
  starting transfers between devices: 76.1 us -> 64.6 us
  waiting for transfers between devices: 94 us -> 98.9 us
    all_to_all x4, waiting for transfers between devices: 38.3 us -> 45.5 us  [exchange(): lax.all_to_all(value, 'wide', split_axis=0, concat_axis=0, tiled=True)]
    ppermute x30, starting transfers between devices: 27 us -> 20.6 us  [swap(): return lax.ppermute(value, axis, [(i, i ^ mask) for i in range(count)])]
    all_gather x1, waiting for transfers between devices: 4.31 us -> 0.02 us  [body(): lax.all_gather(mix_out_low, ('wide', 'tensor'), axis=0, tiled=True)]
  transfers between devices with their start and end apart: 40 -> 40, of which waited for: 12 -> 12; matrix products, arithmetic and copies ran while one was open for 30% -> 31% of each run, Pallas kernels for 21% -> 21%
where the time goes in v3:
time: 408 us; the launch traced here: 400 us
  waiting for transfers between devices  98.9 us (24%)
  Pallas kernels  84.9 us (21%)
  starting transfers between devices  64.6 us (16%)
  other arithmetic  54.7 us (13%)
  matrix products  51.7 us (13%)
  local copies, waits for them, and re-layouts  29.1 us (7%)
  between operations  15.8 us (4%)
    ppermute x30, waiting for transfers between devices, swap(): return lax.ppermute(value, axis, [(i, i ^ mask) for i in range(count)])  52.9 us
    all_to_all x4, waiting for transfers between devices, exchange(): lax.all_to_all(value, 'wide', split_axis=0, concat_axis=0, tiled=True)  45.5 us
    pallas_call x2, Pallas kernels, branch_rows(): pl.pallas_call(functools.partial(branch_rows_kernel, len(chunks)), grid=(...  33.7 us
    pallas_call x2, Pallas kernels, branch_grads(): pl.pallas_call(branch_grads_kernel, grid=(chunks, width // block), in_spe...  21.3 us
    ppermute x30, starting transfers between devices, swap(): return lax.ppermute(value, axis, [(i, i ^ mask) for i in range(count)])  20.6 us
    all_to_all x4, starting transfers between devices, exchange(): lax.all_to_all(value, 'wide', split_axis=0, concat_axis=0, tiled=True)  19.9 us
    unnamed x204, local copies, waits for them, and re-layouts  15 us
    dot_general x6, matrix products, dot(): return jnp.dot(a, b, preferred_element_type=FULL)  13.6 us
  transfers between devices with their start and end apart: 40, of which 12 were waited for; matrix products, arithmetic and copies ran while one was open for 31% of the time, Pallas kernels for 21%

profile of v3, /device:TPU:3, one launch (start us, length us, event | category | flops | bytes accessed | tf_op | source)
XLA Modules:
  0.0 399.8 jit_solution(12230033046618137210)
XLA Ops:
  13.0 6.5 %all-to-all-start = ((bf16[32,24,578]{2,1,0:T(8,128)(2,1)}), bf16[32,24,578]{2,1,0:T(8,128)(2,1)}, u32[]{:S(2)}, u32[]{:S(2)}) async-start(bf16[32,24,578]{2,1,0:T(8,128)(2,1)} %bitcast.148), calls=%async_computation | async-start | bytes 1966080 | tf_op jit(solution)/shard_map/all_to_all | solution.py:436
  52.2 5.0 %all-to-all-start.1 = ((bf16[8,128,768]{2,1,0:T(8,128)(2,1)}), bf16[8,128,768]{2,1,0:T(8,128)(2,1)}, u32[]{:S(2)}, u32[]{:S(2)}) async-start(bf16[8,128,768]{2,1,0:T(8,128)(2,1)} %bitcast.145), calls=%async_computation.1 | async-start | bytes 3145728 | tf_op jit(solution)/shard_map/all_to_all | solution.py:381
  76.2 11.9 %collective-permute-done.3 = bf16[256,192]{0,1:T(8,128)(2,1)S(1)} collective-permute-done((bf16[256,192]{0,1:T(8,128)(2,1)}, bf16[256,192]{0,1:T(8,128)(2,1)S(1)}, u32[]{:S(2)}, u32[]{:S(2)}) %collective-permute-start.3) | collective-permute-done | bytes 98336 | tf_op jit(solution)/shard_map/ppermute | solution.py:335
  96.9 4.7 %all-to-all-start.2 = ((bf16[8,128,768]{2,1,0:T(8,128)(2,1)}), bf16[8,128,768]{2,1,0:T(8,128)(2,1)}, u32[]{:S(2)}, u32[]{:S(2)}) async-start(bf16[8,128,768]{2,1,0:T(8,128)(2,1)} %bitcast.157), calls=%async_computation.2 | async-start | bytes 3145728 | tf_op jit(solution)/shard_map/all_to_all | solution.py:381
  104.7 8.2 %collective-permute-done.11 = bf16[256,768]{1,0:T(8,128)(2,1)S(1)} collective-permute-done((bf16[256,768]{1,0:T(8,128)(2,1)S(1)}, bf16[256,768]{1,0:T(8,128)(2,1)S(1)}, u32[]{:S(2)}, u32[]{:S(2)}) %collective-permute-start.11) | collective-permute-done | bytes 393248 | tf_op jit(solution)/shard_map/ppermute | solution.py:335
  115.0 6.4 %collective-permute-done.8 = bf16[256,768]{1,0:T(8,128)(2,1)S(1)} collective-permute-done((bf16[256,768]{1,0:T(8,128)(2,1)S(1)}, bf16[256,768]{1,0:T(8,128)(2,1)S(1)}, u32[]{:S(2)}, u32[]{:S(2)}) %collective-permute-start.8) | collective-permute-done | bytes 393248 | tf_op jit(solution)/shard_map/ppermute | solution.py:335
  125.1 38.3 %all-to-all-done.2 = bf16[8,128,768]{2,1,0:T(8,128)(2,1)} async-done(((bf16[8,128,768]{2,1,0:T(8,128)(2,1)}), bf16[8,128,768]{2,1,0:T(8,128)(2,1)}, u32[]{:S(2)}, u32[]{:S(2)}) %all-to-all-start.2) | async-done | bytes 1572896 | tf_op jit(solution)/shard_map/all_to_all | solution.py:381
  163.4 25.0 %branch_rows.2 = (bf16[1024,2048]{1,0:T(8,128)(2,1)}, bf16[1024,2048]{1,0:T(8,128)(2,1)}, bf16[1024,2048]{1,0:T(8,128)(2,1)}, bf16[1024,768]{1,0:T(8,128)(2,1)S(...) custom-call(bf16[1024,768]{1,0:T(8,128)(2,1)} %bitcast.21.x_ref, bf16[1024,768]{1,0:T(8,128)(2,1)} %bitcast.19.g_ref, ...), custom_call_target="tpu_custom_call" | custom-call | flops 1000 | bytes 1000 | tf_op jit(solution)/shard_map/branch_rows/pallas_call | solution.py:149
  194.1 8.6 %branch_rows.3 = (bf16[1024,512]{1,0:T(8,128)(2,1)S(1)}, bf16[1024,512]{1,0:T(8,128)(2,1)S(1)}, bf16[1024,512]{1,0:T(8,128)(2,1)S(1)}, bf16[1024,768]{1,0:T(8,12...) custom-call(bf16[1024,768]{1,0:T(8,128)(2,1)} %pad_maximum_fusion.3.x_ref, ...), custom_call_target="tpu_custom_call" | custom-call | flops 1000 | bytes 1000 | tf_op jit(solution)/shard_map/branch_rows/pallas_call | solution.py:149
  202.7 10.9 %branch_grads.3 = bf16[2,3,768,512]{3,2,1,0:T(8,128)(2,1)} custom-call(bf16[768,1024]{1,0:T(8,128)(2,1)S(1)} %get-tuple-element.96.xt_ref, bf16[768,1024]{1,0:T(8,128)(2,1)S(1)} %get-tuple-element.97.gt_ref, bf16[1024,2048]{1,0:T(8,128)(2,1)} %get-tuple-element.95.hidden_ref, bf16[1024,2048]{1,0:T(8,128)(2,1)} %get-tuple-element.98.ggate_ref, ...), custom_call_target="tpu_custom_call" | custom-call | flops 1000 | bytes 1000 | tf_op jit(solution)/shard_map/branch_grads/pallas_call | solution.py:208
  229.4 10.4 %branch_grads.2.refs_0_ = bf16[2,3,768,512]{3,2,1,0:T(8,128)(2,1)} custom-call(bf16[768,1024]{1,0:T(8,128)(2,1)S(1)} %get-tuple-element.96.xt_ref, bf16[768,1024]{1,0:T(8,128)(2,1)S(1)} %get-tuple-element.97.gt_ref, bf16[1024,2048]{1,0:T(8,128)(2,1)} %get-tuple-element.95.hidden_ref, bf16[1024,2048]{1,0:T(8,128)(2,1)} %get-tuple-element.98.ggate_ref, ...), custom_call_target="tpu_custom_call" | custom-call | flops 1000 | bytes 1000 | tf_op jit(solution)/shard_map/branch_grads/pallas_call | solution.py:208
  239.8 5.1 %shared_grads.1 = bf16[8,3,96,512]{3,2,1,0:T(8,128)(2,1)} custom-call(bf16[768,1024]{1,0:T(8,128)(2,1)S(1)} %copy-done.13, bf16[768,1024]{1,0:T(8,128)(2,1)} %get-tuple-element.101.gt_ref, bf16[1024,512]{1,0:T(8,128)(2,1)S(1)} %get-tuple-element.102.hidden_ref, bf16[1024,512]{1,0:T(8,128)(2,1)S(1)} %get-tuple-element.103.ggate_ref, ...), custom_call_target="tpu_custom_call" | custom-call | flops 1000 | bytes 1000 | tf_op jit(solution)/shard_map/shared_grads/pallas_call | solution.py:245
  244.9 7.3 %branch_out.2 = bf16[1024,768]{1,0:T(8,128)(2,1)} custom-call(bf16[1024,2048]{1,0:T(8,128)(2,1)} %get-tuple-element.95.hidden_ref, bf16[3,768,512]{2,1,0:T(8,128)(2,1)S(1)} %copy-done.3, bf16[3,768,512]{2,1,0:T(8,128)(2,1)} %collective-permute-done.6.refs_1_, bf16[3,768,512]{2,1,0:T(8,128)(2,1)} %collective-permute-done.13.refs_2_, ...), custom_call_target="tpu_custom_call" | custom-call | flops 1000 | bytes 1000 | tf_op jit(solution)/shard_map/branch_out/pallas_call | solution.py:178
  258.6 8.8 %collective-permute-done.22 = bf16[256,768]{1,0:T(8,128)(2,1)S(1)} collective-permute-done((bf16[256,768]{1,0:T(8,128)(2,1)S(1)}, bf16[256,768]{1,0:T(8,128)(2,1)S(1)}, u32[]{:S(2)}, u32[]{:S(2)}) %collective-permute-start.22) | collective-permute-done | bytes 393248 | tf_op jit(solution)/shard_map/ppermute | solution.py:335
  268.7 5.7 %all-to-all-start.4 = ((bf16[8,128,768]{2,1,0:T(8,128)(2,1)}), bf16[8,128,768]{2,1,0:T(8,128)(2,1)}, u32[]{:S(2)}, u32[]{:S(2)}) async-start(bf16[8,128,768]{2,1,0:T(8,128)(2,1)} %bitcast.27), calls=%async_computation.4 | async-start | bytes 3145728 | tf_op jit(solution)/shard_map/all_to_all | solution.py:381
  287.7 6.7 %multiply_reduce_fusion = (f32[3,1024]{1,0:T(4,128)S(1)}, f32[3,1024,1024]{1,2,0:T(8,128)S(1)}) fusion(f32[3,1024,1024]{1,2,0:T(8,128)} %copy-done.15, f32[3,1024]{1,0:T(4,128)S(1)} %log_add_fusion, bf16[1024,3,64]{0,2,1:T(8,128)(2,1)S(1)} %bitcast.155, f32[1024,3,3,64]{0,3,2,1:T(8,128)} %bitcast.154), kind=kOutput, calls=%fused_computation.1 | convolution fusion | flops 412087296 | bytes 25976832 | tf_op jit(solution)/shard_map/qhd,khd->hqk/dot_general | solution.py:101
  295.3 5.2 %multiply_convert_fusion = bf16[3,1024,1024]{1,2,0:T(8,128)(2,1)} fusion(f32[3,1024,1024]{1,2,0:T(8,128)S(1)} %get-tuple-element.212, f32[3,1024,1024]{1,2,0:T(8,128)S(1)} %bitcast.143, f32[3,1024]{1,0:T(4,128)S(1)} %get-tuple-element.211, f32[3,1024]{1,0:T(4,128)S(1)} %log_add_fusion), kind=kLoop, calls=%fused_computation | loop fusion | flops 12582912 | bytes 31481856 | tf_op jit(solution)/shard_map/convert_element_type | solution.py:103
  300.6 5.0 %fusion.12 = f32[1024,3,64]{0,2,1:T(8,128)S(1)} fusion(bf16[3,1024,1024]{1,2,0:T(8,128)(2,1)} %multiply_convert_fusion, bf16[1024,3,32]{0,2,1:T(8,128)(2,1)S(1)} %copy-done.57, bf16[1024,3,32]{0,2,1:T(8,128)(2,1)S(1)} %copy-done.55), kind=kOutput, calls=%fused_computation.40 | convolution fusion | flops 403636224 | bytes 7471104 | tf_op jit(solution)/shard_map/hqk,qhd->khd/dot_general | solution.py:105
  318.2 7.2 %all-to-all-done.4 = bf16[8,128,768]{2,1,0:T(8,128)(2,1)} async-done(((bf16[8,128,768]{2,1,0:T(8,128)(2,1)}), bf16[8,128,768]{2,1,0:T(8,128)(2,1)}, u32[]{:S(2)}, u32[]{:S(2)}) %all-to-all-start.4) | async-done | bytes 1572896 | tf_op jit(solution)/shard_map/all_to_all | solution.py:381
  329.5 11.0 %all-to-all-start.5 = ((bf16[32,24,577]{2,1,0:T(8,128)(2,1)}), bf16[32,24,577]{2,1,0:T(8,128)(2,1)}, u32[]{:S(2)}, u32[]{:S(2)}) async-start(bf16[32,24,577]{2,1,0:T(8,128)(2,1)} %pad_maximum_fusion.7), calls=%async_computation.5 | async-start | bytes 1966080 | tf_op jit(solution)/shard_map/all_to_all | solution.py:597
  345.2 10.2 %adam_in.1 = (f32[6144,128]{1,0:T(8,128)}, f32[6144,128]{1,0:T(8,128)}, f32[6144,128]{1,0:T(8,128)}) custom-call(bf16[2,3,768,512]{3,2,1,0:T(8,128)(2,1)} %branch_grads.2.refs_0_, bf16[2,3,768,512]{3,2,1,0:T(8,128)(2,1)} %collective-permute-done.18.refs_1_, bf16[1,2,768,512]{3,2,1,0:T(8,128)(2,1)S(1)} %bitcast.139, f32[6144,128]{1,0:T(8,128)S(1)} %bitcast.138, ...), custom_call_target="tpu_custom_call" | custom-call | flops 1000 | bytes 1000 | tf_op jit(solution)/shard_map/adam_in/pallas_call | solution.py:289
  361.2 8.4 %collective-permute-done.29 = bf16[1,768,512]{2,1,0:T(8,128)(2,1)S(1)} collective-permute-done((bf16[1,768,512]{2,1,0:T(8,128)(2,1)S(1)}, bf16[1,768,512]{2,1,0:T(8,128)(2,1)S(1)}, u32[]{:S(2)}, u32[]{:S(2)}) %collective-permute-start.29) | collective-permute-done | bytes 786464 | tf_op jit(solution)/shard_map/ppermute | solution.py:335
  369.6 5.8 %adam_out.1 = (f32[1,512,768]{2,1,0:T(8,128)}, f32[1,512,768]{2,1,0:T(8,128)}, f32[1,512,768]{2,1,0:T(8,128)}) custom-call(bf16[2,3,768,512]{3,2,1,0:T(8,128)(2,1)} %branch_grads.2.refs_0_, bf16[2,3,768,512]{3,2,1,0:T(8,128)(2,1)} %collective-permute-done.18.refs_1_, bf16[1,1,768,512]{3,2,1,0:T(8,128)(2,1)S(1)} %bitcast.141, f32[1,512,768]{2,1,0:T(8,128)S(1)} %copy-done.7, ...), custom_call_target="tpu_custom_call" | custom-call | flops 1000 | bytes 1000 | tf_op jit(solution)/shard_map/adam_out/pallas_call | solution.py:322
  381.6 6.1 %collective-permute-start.30 = (bf16[24,768]{1,0:T(8,128)(2,1)S(1)}, bf16[24,768]{1,0:T(8,128)(2,1)S(1)}, u32[]{:S(2)}, u32[]{:S(2)}) collective-permute-start(bf16[24,768]{1,0:T(8,128)(2,1)S(1)} %reshape.500), channel_id=1, source_target_pairs={{0,0},{1,8},{2,16},{3,24},{4,1},{5,9},{6,17},{7,25},{8,2},{9,10},{... | collective-permute-start | bytes 110600 | tf_op jit(solution)/shard_map/ppermute | solution.py:612
  (381 shorter events, 155.7 us)
Async XLA Ops:
  7.2 84.2 %all-gather.3.cloned.1.call-start = ((), (), s32[]{:S(2)}) async-start(), calls=%async_computation.7 | async-start | bytes 1216512 | tf_op jit(solution)/shard_map/all_gather | solution.py:453
  7.3 27.5 %collective-permute-start = (bf16[256,768]{1,0:T(8,128)(2,1)}, bf16[256,768]{1,0:T(8,128)(2,1)}, u32[]{:S(2)}, u32[]{:S(2)}) collective-permute-start(bf16[256,768]{1,0:T(8,128)(2,1)} %param.26), channel_id=1, source_target_pairs={{0,2},{1,3},{2,0},{3,1},{4,6},{5,7},{6,4},{7,5},{8,10},{9,11},{10,... | collective-permute-start | bytes 1179656 | tf_op jit(solution)/shard_map/ppermute | solution.py:335
  7.3 34.1 %collective-permute-start.2 = (bf16[256,768]{1,0:T(8,128)(2,1)}, bf16[256,768]{1,0:T(8,128)(2,1)}, u32[]{:S(2)}, u32[]{:S(2)}) collective-permute-start(bf16[256,768]{1,0:T(8,128)(2,1)} %param.26), channel_id=1, source_target_pairs={{0,1},{1,0},{2,3},{3,2},{4,5},{5,4},{6,7},{7,6},{8,9},{9,8},{10,11... | collective-permute-start | bytes 1179656 | tf_op jit(solution)/shard_map/ppermute | solution.py:335
  13.0 32.2 %all-to-all-start = ((bf16[32,24,578]{2,1,0:T(8,128)(2,1)}), bf16[32,24,578]{2,1,0:T(8,128)(2,1)}, u32[]{:S(2)}, u32[]{:S(2)}) async-start(bf16[32,24,578]{2,1,0:T(8,128)(2,1)} %bitcast.148), calls=%async_computation | async-start | bytes 1966080 | tf_op jit(solution)/shard_map/all_to_all | solution.py:436
  24.5 67.0 %collective-permute-start.6 = (bf16[3,768,512]{2,1,0:T(8,128)(2,1)S(1)}, bf16[3,768,512]{2,1,0:T(8,128)(2,1)}, u32[]{:S(2)}, u32[]{:S(2)}) collective-permute-start(bf16[3,768,512]{2,1,0:T(8,128)(2,1)S(1)} %pad_maximum_fusion.1.refs_0_), channel_id=1, source_target_pairs={{0,2},{1,3},{2,0},{3,1},{4,6},{5,7},{6,4},{7,5},{8,10},{9,11},{10,... | collective-permute-start | bytes 7077896 | tf_op jit(solution)/shard_map/ppermute | solution.py:335
  52.2 44.6 %all-to-all-start.1 = ((bf16[8,128,768]{2,1,0:T(8,128)(2,1)}), bf16[8,128,768]{2,1,0:T(8,128)(2,1)}, u32[]{:S(2)}, u32[]{:S(2)}) async-start(bf16[8,128,768]{2,1,0:T(8,128)(2,1)} %bitcast.145), calls=%async_computation.1 | async-start | bytes 3145728 | tf_op jit(solution)/shard_map/all_to_all | solution.py:381
  57.2 136.8 %all-gather.5.cloned.1.call-start = ((), (), s32[]{:S(2)}) async-start(), calls=%async_computation.8 | async-start | bytes 2654208 | tf_op jit(solution)/shard_map/all_gather | solution.py:455
  96.9 66.5 %all-to-all-start.2 = ((bf16[8,128,768]{2,1,0:T(8,128)(2,1)}), bf16[8,128,768]{2,1,0:T(8,128)(2,1)}, u32[]{:S(2)}, u32[]{:S(2)}) async-start(bf16[8,128,768]{2,1,0:T(8,128)(2,1)} %bitcast.157), calls=%async_computation.2 | async-start | bytes 3145728 | tf_op jit(solution)/shard_map/all_to_all | solution.py:381
  101.6 61.8 %collective-permute-start.13 = (bf16[3,768,512]{2,1,0:T(8,128)(2,1)S(1)}, bf16[3,768,512]{2,1,0:T(8,128)(2,1)}, u32[]{:S(2)}, u32[]{:S(2)}) collective-permute-start(bf16[3,768,512]{2,1,0:T(8,128)(2,1)S(1)} %pad_maximum_fusion.1.refs_0_), channel_id=1, source_target_pairs={{0,1},{1,0},{2,3},{3,2},{4,5},{5,4},{6,7},{7,6},{8,9},{9,8},{10,11... | collective-permute-start | bytes 7077896 | tf_op jit(solution)/shard_map/ppermute | solution.py:335
  102.5 60.9 %collective-permute-start.14 = (bf16[3,768,512]{2,1,0:T(8,128)(2,1)}, bf16[3,768,512]{2,1,0:T(8,128)(2,1)}, u32[]{:S(2)}, u32[]{:S(2)}) collective-permute-start(bf16[3,768,512]{2,1,0:T(8,128)(2,1)} %collective-permute-done.6.refs_1_), channel_id=1, source_target_pairs={{0,1},{1,0},{2,3},{3,2},{4,5},{5,4},{6,7},{7,6},{8,9},{9,8},{10,11... | collective-permute-start | bytes 7077896 | tf_op jit(solution)/shard_map/ppermute | solution.py:335
  189.6 63.7 %all-to-all-start.3 = ((bf16[8,128,768]{2,1,0:T(8,128)(2,1)}), bf16[8,128,768]{2,1,0:T(8,128)(2,1)}, u32[]{:S(2)}, u32[]{:S(2)}) async-start(bf16[8,128,768]{2,1,0:T(8,128)(2,1)} %bitcast.140), calls=%async_computation.3 | async-start | bytes 3145728 | tf_op jit(solution)/shard_map/all_to_all | solution.py:381
  213.6 68.8 %collective-permute-start.18 = (bf16[2,3,768,512]{3,2,1,0:T(8,128)(2,1)}, bf16[2,3,768,512]{3,2,1,0:T(8,128)(2,1)}, u32[]{:S(2)}, u32[]{:S(2)}) collective-permute-start(bf16[2,3,768,512]{3,2,1,0:T(8,128)(2,1)} %branch_grads.3), channel_id=1, source_target_pairs={{0,1},{1,0},{2,3},{3,2},{4,5},{5,4},{6,7},{7,6},{8,9},{9,8},{10,11... | collective-permute-start | bytes 14155784 | tf_op jit(solution)/shard_map/ppermute | solution.py:335
  217.1 35.1 %collective-permute-start.17 = (bf16[256,768]{1,0:T(8,128)(2,1)S(1)}, bf16[256,768]{1,0:T(8,128)(2,1)S(1)}, u32[]{:S(2)}, u32[]{:S(2)}) collective-permute-start(bf16[256,768]{1,0:T(8,128)(2,1)S(1)} %get-tuple-element.174), channel_id=1, source_target_pairs={{0,3},{1,2},{2,1},{3,0},{4,7},{5,6},{6,5},{7,4},{8,11},{9,10},{10,... | collective-permute-start | bytes 1179656 | tf_op jit(solution)/shard_map/ppermute | solution.py:335
  220.0 33.3 %collective-permute-start.19 = (bf16[256,768]{1,0:T(8,128)(2,1)}, bf16[256,768]{1,0:T(8,128)(2,1)}, u32[]{:S(2)}, u32[]{:S(2)}) collective-permute-start(bf16[256,768]{1,0:T(8,128)(2,1)} %get-tuple-element.170), channel_id=1, source_target_pairs={{0,1},{1,0},{2,3},{3,2},{4,5},{5,4},{6,7},{7,6},{8,9},{9,8},{10,11... | collective-permute-start | bytes 1179656 | tf_op jit(solution)/shard_map/ppermute | solution.py:335
  223.7 29.6 %collective-permute-start.20 = (bf16[256,768]{1,0:T(8,128)(2,1)}, bf16[256,768]{1,0:T(8,128)(2,1)}, u32[]{:S(2)}, u32[]{:S(2)}) collective-permute-start(bf16[256,768]{1,0:T(8,128)(2,1)} %get-tuple-element.172), channel_id=1, source_target_pairs={{0,2},{1,3},{2,0},{3,1},{4,6},{5,7},{6,4},{7,5},{8,10},{9,11},{10,... | collective-permute-start | bytes 1179656 | tf_op jit(solution)/shard_map/ppermute | solution.py:335
  227.1 26.2 %collective-permute-start.21 = (bf16[256,768]{1,0:T(8,128)(2,1)}, bf16[256,768]{1,0:T(8,128)(2,1)}, u32[]{:S(2)}, u32[]{:S(2)}) collective-permute-start(bf16[256,768]{1,0:T(8,128)(2,1)} %get-tuple-element.171), channel_id=1, source_target_pairs={{0,3},{1,2},{2,1},{3,0},{4,7},{5,6},{6,5},{7,4},{8,11},{9,10},{10,... | collective-permute-start | bytes 1179656 | tf_op jit(solution)/shard_map/ppermute | solution.py:335
  268.7 56.8 %all-to-all-start.4 = ((bf16[8,128,768]{2,1,0:T(8,128)(2,1)}), bf16[8,128,768]{2,1,0:T(8,128)(2,1)}, u32[]{:S(2)}, u32[]{:S(2)}) async-start(bf16[8,128,768]{2,1,0:T(8,128)(2,1)} %bitcast.27), calls=%async_computation.4 | async-start | bytes 3145728 | tf_op jit(solution)/shard_map/all_to_all | solution.py:381
  274.4 105.3 %reduce-scatter.2.cloned.1.call-start = ((), (), s32[]{:S(2)}) async-start(), calls=%async_computation.9 | async-start | bytes 3022848 | tf_op jit(solution)/shard_map/reduce_scatter | solution.py:552
  287.7 37.8 %collective-permute-start.28 = (bf16[2,768,512]{2,1,0:T(8,128)(2,1)}, bf16[2,768,512]{2,1,0:T(8,128)(2,1)S(1)}, u32[]{:S(2)}, u32[]{:S(2)}) collective-permute-start(bf16[2,768,512]{2,1,0:T(8,128)(2,1)} %slice_bitcast_fusion), channel_id=1, source_target_pairs={{0,2},{1,3},{2,0},{3,1},{4,6},{5,7},{6,4},{7,5},{8,10},{9,11},{10,... | collective-permute-start | bytes 4718600 | tf_op jit(solution)/shard_map/ppermute | solution.py:335
  313.9 41.4 %collective-permute-start.25 = (bf16[256,768]{1,0:T(8,128)(2,1)}, bf16[256,768]{1,0:T(8,128)(2,1)}, u32[]{:S(2)}, u32[]{:S(2)}) collective-permute-start(bf16[256,768]{1,0:T(8,128)(2,1)} %get-tuple-element.164), channel_id=1, source_target_pairs={{0,1},{1,0},{2,3},{3,2},{4,5},{5,4},{6,7},{7,6},{8,9},{9,8},{10,11... | collective-permute-start | bytes 1179656 | tf_op jit(solution)/shard_map/ppermute | solution.py:335
  314.2 41.1 %collective-permute-start.26 = (bf16[256,768]{1,0:T(8,128)(2,1)}, bf16[256,768]{1,0:T(8,128)(2,1)}, u32[]{:S(2)}, u32[]{:S(2)}) collective-permute-start(bf16[256,768]{1,0:T(8,128)(2,1)} %get-tuple-element.163), channel_id=1, source_target_pairs={{0,2},{1,3},{2,0},{3,1},{4,6},{5,7},{6,4},{7,5},{8,10},{9,11},{10,... | collective-permute-start | bytes 1179656 | tf_op jit(solution)/shard_map/ppermute | solution.py:335
  315.5 39.9 %collective-permute-start.27 = (bf16[256,768]{1,0:T(8,128)(2,1)}, bf16[256,768]{1,0:T(8,128)(2,1)}, u32[]{:S(2)}, u32[]{:S(2)}) collective-permute-start(bf16[256,768]{1,0:T(8,128)(2,1)} %get-tuple-element.162), channel_id=1, source_target_pairs={{0,3},{1,2},{2,1},{3,0},{4,7},{5,6},{6,5},{7,4},{8,11},{9,10},{10,... | collective-permute-start | bytes 1179656 | tf_op jit(solution)/shard_map/ppermute | solution.py:335
  329.5 46.0 %all-to-all-start.5 = ((bf16[32,24,577]{2,1,0:T(8,128)(2,1)}), bf16[32,24,577]{2,1,0:T(8,128)(2,1)}, u32[]{:S(2)}, u32[]{:S(2)}) async-start(bf16[32,24,577]{2,1,0:T(8,128)(2,1)} %pad_maximum_fusion.7), calls=%async_computation.5 | async-start | bytes 1966080 | tf_op jit(solution)/shard_map/all_to_all | solution.py:597
  344.9 24.7 %collective-permute-start.29 = (bf16[1,768,512]{2,1,0:T(8,128)(2,1)S(1)}, bf16[1,768,512]{2,1,0:T(8,128)(2,1)S(1)}, u32[]{:S(2)}, u32[]{:S(2)}) collective-permute-start(bf16[1,768,512]{2,1,0:T(8,128)(2,1)S(1)} %copy-done.47), channel_id=1, source_target_pairs={{0,2},{1,3},{2,0},{3,1},{4,6},{5,7},{6,4},{7,5},{8,10},{9,11},{10,... | collective-permute-start | bytes 2359304 | tf_op jit(solution)/shard_map/ppermute | solution.py:335
  (116 other events, 988.3 us)
Sparse Core Ops, SparseCore 0:
  11.5 62.8 all-gather.2
  91.6 75.8 all-gather.4
  282.5 95.2 reduce-scatter.1
